TPU v7x, 768 devices: a whole 4x8x12 slice. The times are simulated.
768 devices in a mesh: row: 8 (over z_lo, core), col: 12 (over z_hi, x), depth: 8 (over y).
Axes of the slice: x: 4, y: 8, z: 12 (z_hi: 3, z_lo: 4; z = z_hi * 4 + z_lo), core: 2. Of those that a mesh axis runs over, the one named last changes fastest.
Arguments:
- left_blocks: float32 [12288, 64, 64], P(('row', 'col', 'depth')), may hold values from -6 to 6
- right_blocks: float32 [12288, 64, 64], P(('row', 'col', 'depth')), may hold values from -0.125 to 0.125
- triples: int32 [3, 393216], P(None, ('row', 'col', 'depth')), may hold values from 0 to 191, as said below
Outputs:
- product_blocks: float32 [12288, 64, 64], P(('row', 'col', 'depth'))
Inputs may be any that keep to these rules, and one draw needn't show every extreme that they name: With G = 4 contraction groups per panel and layer, left slot number i * G + g is the block of block row i and group g, and right slot j * G + g the block of group g and block column j. Each device keeps 128 distinct (block row, block column) pairs, and out slot o names the o-th of them. A used triple takes the left block (i, g) and the right block (g, j) of one group g and sends their product to the kept slot of (i, j); a device's used triples are distinct and come first among its 512. An unused triple is (0, 0, 128). Every device has at least 128 used triples, and some device has all 512 used.
All inputs are finite; a program needn't handle non-finite values.
Results may differ from a plain program's by a relative error of at most 0.0003.
Values sent between devices are 32-bit elements; how exact they have to be, the bound alone decides.
No kernel may reach another device: no remote copies, remote signals or barrier semaphores. Data moves between devices by JAX's collectives and lax.ppermute only.
A program may use at most 128 MiB of HBM per device.

v0:
```python
import math

import jax
import jax.numpy as jnp
from jax import lax
from jax.sharding import PartitionSpec as P

PC = 128


def per_device(left_blocks, right_blocks, triples):
    order = left_blocks.shape[1]
    left_panel = lax.all_gather(left_blocks, "col", axis=0, tiled=True)
    right_panel = lax.all_gather(right_blocks, "row", axis=0, tiled=True)
    slot_count = triples.shape[1]
    group_size = math.gcd(slot_count, 128)
    left_slots = triples[0]
    right_slots = triples[1]
    out_slots = triples[2]

    def accumulate(step_index, partial_value):
        start = step_index * group_size
        left_pick = lax.dynamic_slice_in_dim(left_slots, start, group_size)
        right_pick = lax.dynamic_slice_in_dim(right_slots, start, group_size)
        out_pick = lax.dynamic_slice_in_dim(out_slots, start, group_size)
        products = jnp.einsum(
            "tij,tjk->tik",
            left_panel[left_pick],
            right_panel[right_pick],
            precision=lax.Precision.HIGHEST,
            preferred_element_type=jnp.float32,
        )
        return partial_value.at[out_pick].add(products)

    partial_value = jnp.zeros((PC + 1, order, order), jnp.float32)
    partial_value = lax.fori_loop(0, slot_count // group_size, accumulate, partial_value)
    partial_value = partial_value[:PC]
    layers = lax.axis_size("depth")
    share = PC // layers
    summed = lax.psum(partial_value, "depth")
    kept = lax.dynamic_slice_in_dim(summed, lax.axis_index("depth") * share, share, 0)
    return kept


def solution(mesh):
    placed = (
        P(("row", "col", "depth"), None, None),
        P(("row", "col", "depth"), None, None),
        P(None, ("row", "col", "depth")),
    )
    return jax.shard_map(
        per_device,
        mesh=mesh,
        in_specs=placed,
        out_specs=P(("row", "col", "depth"), None, None),
        check_vma=False,
    )
```

profile of v0, /device:TPU:1, one launch (start us, length us, event | category | flops | bytes accessed | tf_op | source)
XLA Modules:
  0.0 552.0 jit_solution(2121363844166082154)
XLA Ops:
  6.5 0.0 all-gather.5.cloned.1.call-start
  6.5 0.7 all-gather.5.cloned.1.call-update
  7.3 0.0 all-gather.3.cloned.1.call-start
  7.3 0.7 all-gather.3.cloned.1.call-update
  8.0 0.0 all-reduce.2.cloned.1.call-start
  8.1 0.8 fusion
  8.9 66.2 %all-gather.5.cloned.1.call-done = f32[128,64,64]{2,1,0:T(8,128)} async-done(((f32[16,64,64]{2,1,0:T(8,128)}), f32[128,64,64]{2,1,0:T(8,128)}) %all-gather.5.cloned.1.call-update) | async-done | bytes 2097168 | tf_op jit(solution)/shard_map/all_gather | solution.py:14
  75.1 156.2 %all-gather.3.cloned.1.call-done = f32[192,64,64]{2,1,0:T(8,128)} async-done(((f32[16,64,64]{2,1,0:T(8,128)}), f32[192,64,64]{2,1,0:T(8,128)}) %all-gather.3.cloned.1.call-update) | async-done | bytes 3145744 | tf_op jit(solution)/shard_map/all_gather | solution.py:13
  231.3 2.6 broadcast_in_dim.24
  233.8 168.3 %while.13 = (s32[]{:T(128)}, f32[129,64,64]{2,1,0:T(8,128)}, s32[512]{0:T(512)S(1)}, s32[512]{0:T(512)S(1)}, f32[192,64,64]{2,1,0:T(8,128)}, /*index=5*/s32[512]...) while((s32[]{:T(128)}, f32[129,64,64]{2,1,0:T(8,128)}, ...), condition=%wide.region_2.0_spmd, body=%wide.region_0.0_spmd.sunk | while | flops 403180672 | bytes 20985508 | solution.py:36
  233.8 0.1 compare_select_fusion.6
  233.9 5.6 %gather_fusion = f32[128,64,64]{2,1,0:T(8,128)} fusion(f32[192,64,64]{2,1,0:T(8,128)} %get-tuple-element.222, s32[1024]{0:T(1024)S(1)} %pad_clamp_fusion.4), kind=kCustom, calls=%fused_computation.clone.1 | custom fusion | bytes 4194816 | tf_op jit(solution)/shard_map/while/body/eval_jaxpr/gather | solution.py:28
  239.5 5.0 gather_fusion.1
  244.6 9.8 %fusion.9 = f32[128,64,64]{2,1,0:T(8,128)} fusion(f32[128,64,64]{2,1,0:T(8,128)} %gather_fusion, f32[128,64,64]{2,1,0:T(8,128)} %gather_fusion.1), kind=kOutput, calls=%fused_computation.10.clone.1 | convolution fusion | flops 402653184 | bytes 6291456 | tf_op jit(solution)/shard_map/while/body/eval_jaxpr/tij,tjk->tik/dot_general | solution.py:26
  254.4 0.1 compare_select_fusion.5
  254.5 20.3 %scatter_fusion = f32[129,64,64]{2,1,0:T(8,128)} fusion(f32[129,64,64]{2,1,0:T(8,128)} %get-tuple-element.208, s32[128]{0:T(128)S(1)} %compare_select_fusion.5, f32[128,64,64]{2,1,0:T(8,128)} %fusion.9), kind=kCustom, calls=%fused_computation.2.clone.1 | custom fusion | flops 524288 | bytes 6291968 | tf_op jit(solution)/shard_map/while/body/eval_jaxpr/scatter-add | solution.py:33
  274.8 0.1 compare_select_fusion.6
  274.9 5.6 %gather_fusion = f32[128,64,64]{2,1,0:T(8,128)} fusion(f32[192,64,64]{2,1,0:T(8,128)} %get-tuple-element.222, s32[1024]{0:T(1024)S(1)} %pad_clamp_fusion.4), kind=kCustom, calls=%fused_computation.clone.1 | custom fusion | bytes 4194816 | tf_op jit(solution)/shard_map/while/body/eval_jaxpr/gather | solution.py:28
  280.6 5.0 gather_fusion.1
  285.6 9.8 %fusion.9 = f32[128,64,64]{2,1,0:T(8,128)} fusion(f32[128,64,64]{2,1,0:T(8,128)} %gather_fusion, f32[128,64,64]{2,1,0:T(8,128)} %gather_fusion.1), kind=kOutput, calls=%fused_computation.10.clone.1 | convolution fusion | flops 402653184 | bytes 6291456 | tf_op jit(solution)/shard_map/while/body/eval_jaxpr/tij,tjk->tik/dot_general | solution.py:26
  295.4 0.1 compare_select_fusion.5
  295.5 20.4 %scatter_fusion = f32[129,64,64]{2,1,0:T(8,128)} fusion(f32[129,64,64]{2,1,0:T(8,128)} %get-tuple-element.208, s32[128]{0:T(128)S(1)} %compare_select_fusion.5, f32[128,64,64]{2,1,0:T(8,128)} %fusion.9), kind=kCustom, calls=%fused_computation.2.clone.1 | custom fusion | flops 524288 | bytes 6291968 | tf_op jit(solution)/shard_map/while/body/eval_jaxpr/scatter-add | solution.py:33
  315.9 0.1 compare_select_fusion.6
  316.0 5.6 %gather_fusion = f32[128,64,64]{2,1,0:T(8,128)} fusion(f32[192,64,64]{2,1,0:T(8,128)} %get-tuple-element.222, s32[1024]{0:T(1024)S(1)} %pad_clamp_fusion.4), kind=kCustom, calls=%fused_computation.clone.1 | custom fusion | bytes 4194816 | tf_op jit(solution)/shard_map/while/body/eval_jaxpr/gather | solution.py:28
  321.6 5.0 gather_fusion.1
  326.6 9.8 %fusion.9 = f32[128,64,64]{2,1,0:T(8,128)} fusion(f32[128,64,64]{2,1,0:T(8,128)} %gather_fusion, f32[128,64,64]{2,1,0:T(8,128)} %gather_fusion.1), kind=kOutput, calls=%fused_computation.10.clone.1 | convolution fusion | flops 402653184 | bytes 6291456 | tf_op jit(solution)/shard_map/while/body/eval_jaxpr/tij,tjk->tik/dot_general | solution.py:26
  336.5 0.1 compare_select_fusion.5
  336.5 20.4 %scatter_fusion = f32[129,64,64]{2,1,0:T(8,128)} fusion(f32[129,64,64]{2,1,0:T(8,128)} %get-tuple-element.208, s32[128]{0:T(128)S(1)} %compare_select_fusion.5, f32[128,64,64]{2,1,0:T(8,128)} %fusion.9), kind=kCustom, calls=%fused_computation.2.clone.1 | custom fusion | flops 524288 | bytes 6291968 | tf_op jit(solution)/shard_map/while/body/eval_jaxpr/scatter-add | solution.py:33
  356.9 0.1 compare_select_fusion.6
  357.0 5.6 %gather_fusion = f32[128,64,64]{2,1,0:T(8,128)} fusion(f32[192,64,64]{2,1,0:T(8,128)} %get-tuple-element.222, s32[1024]{0:T(1024)S(1)} %pad_clamp_fusion.4), kind=kCustom, calls=%fused_computation.clone.1 | custom fusion | bytes 4194816 | tf_op jit(solution)/shard_map/while/body/eval_jaxpr/gather | solution.py:28
  362.6 5.0 gather_fusion.1
  367.7 9.8 %fusion.9 = f32[128,64,64]{2,1,0:T(8,128)} fusion(f32[128,64,64]{2,1,0:T(8,128)} %gather_fusion, f32[128,64,64]{2,1,0:T(8,128)} %gather_fusion.1), kind=kOutput, calls=%fused_computation.10.clone.1 | convolution fusion | flops 402653184 | bytes 6291456 | tf_op jit(solution)/shard_map/while/body/eval_jaxpr/tij,tjk->tik/dot_general | solution.py:26
  377.5 0.1 compare_select_fusion.5
  377.6 24.6 %scatter_fusion = f32[129,64,64]{2,1,0:T(8,128)} fusion(f32[129,64,64]{2,1,0:T(8,128)} %get-tuple-element.208, s32[128]{0:T(128)S(1)} %compare_select_fusion.5, f32[128,64,64]{2,1,0:T(8,128)} %fusion.9), kind=kCustom, calls=%fused_computation.2.clone.1 | custom fusion | flops 524288 | bytes 6291968 | tf_op jit(solution)/shard_map/while/body/eval_jaxpr/scatter-add | solution.py:33
  402.2 4.7 slice.15
  406.9 0.0 all-reduce.2.cloned.1.call-update
  406.9 136.7 %all-reduce.2.cloned.1.call-done = f32[128,64,64]{2,1,0:T(8,128)} async-done(((f32[128,64,64]{2,1,0:T(8,128)}), f32[128,64,64]{2,1,0:T(8,128)}) %all-reduce.2.cloned.1.call-update) | async-done | bytes 2097168 | tf_op jit(solution)/shard_map/psum | solution.py:40
  543.6 1.9 constant_dynamic-slice_fusion
  (8 shorter events, 0.1 us)
Async XLA Ops:
  6.5 68.5 %all-gather.5.cloned.1.call-start = ((), (), s32[]{:S(2)}) async-start(), calls=%async_computation.1 | async-start | bytes 4718592 | tf_op jit(solution)/shard_map/all_gather | solution.py:14
  7.3 224.0 %all-gather.3.cloned.1.call-start = ((), (), s32[]{:S(2)}) async-start(), calls=%async_computation | async-start | bytes 6815744 | tf_op jit(solution)/shard_map/all_gather | solution.py:13
  8.0 535.6 %all-reduce.2.cloned.1.call-start = ((), (), s32[]{:S(2)}) async-start(), calls=%async_computation.2 | async-start | bytes 8388608 | tf_op jit(solution)/shard_map/psum | solution.py:40
Sparse Core Ops, SparseCore 0:
  9.7 65.3 all-gather.4
  79.1 152.1 all-gather.2
  407.0 136.4 all-reduce.1
where the time goes:
time: 554 us; the launch traced here: 552 us
  waiting for transfers between devices  360 us (65%)
  other arithmetic  86.3 us (16%)
  local copies, waits for them, and re-layouts  52.6 us (9%)
  matrix products  39.3 us (7%)
  between operations  13.1 us (2%)
    all_gather x1, waiting for transfers between devices, per_device(): left_panel = lax.all_gather(left_blocks, 'col', axis=0, tiled=True)  156 us
    psum x1, waiting for transfers between devices, per_device(): summed = lax.psum(partial_value, 'depth')  137 us
    scatter-add x4, other arithmetic, accumulate(): return partial_value.at[out_pick].add(products)  85.7 us
    all_gather x1, waiting for transfers between devices, per_device(): right_panel = lax.all_gather(right_blocks, 'row', axis=0, tiled=True)  66.2 us
    dot_general x4, matrix products, accumulate(): jnp.einsum('tij,tjk->tik', left_panel[left_pick], right_panel[right_pick]...  39.3 us
    gather x4, local copies, waits for them, and re-layouts, accumulate(): left_panel[left_pick]  22.6 us
    gather x4, local copies, waits for them, and re-layouts, accumulate(): right_panel[right_pick]  20.1 us
  transfers between devices with their start and end apart: 3, of which 3 were waited for; matrix products, arithmetic and copies ran while one was open for 0% of the time, Pallas kernels for 0%

commit v1 on v0

v1 whole, which is shorter than its diff:
```python
import jax
import jax.numpy as jnp
from jax import lax
from jax.experimental import pallas as pl
from jax.experimental.pallas import tpu as pltpu
from jax.sharding import PartitionSpec as P

BS = 64
GROUPS = 4
SLOTS = 512
PC = 128
LAYERS = 8
SHARE = PC // LAYERS
VM = pl.BlockSpec(memory_space=pltpu.VMEM)
SM = pl.BlockSpec(memory_space=pltpu.SMEM)
F32 = jnp.float32
BF16 = jnp.bfloat16


def params():
    return pltpu.CompilerParams(vmem_limit_bytes=32 * 2**20)


def cost(flops, nbytes):
    return pl.CostEstimate(flops=flops, bytes_accessed=nbytes, transcendentals=0)


def pack_kernel(l_ref, r_ref, lp_ref, rp_ref):
    for i in range(4):
        for h in range(2):
            lp_ref[i * 64 : (i + 1) * 64, h * 128 : (h + 1) * 128] = jnp.concatenate(
                [l_ref[4 * i + 2 * h], l_ref[4 * i + 2 * h + 1]], axis=1
            )
    for g in range(GROUPS):
        for h in range(2):
            rp_ref[g * 64 : (g + 1) * 64, h * 128 : (h + 1) * 128] = jnp.concatenate(
                [r_ref[8 * h + g], r_ref[8 * h + 4 + g]], axis=1
            )


def pack(l, r):
    o = jax.ShapeDtypeStruct((256, 256), F32)
    return pl.pallas_call(
        pack_kernel, out_shape=(o, o), in_specs=[VM, VM], out_specs=(VM, VM), compiler_params=params(), cost_estimate=cost(0, 2**21)
    )(l, r)


def table_kernel(t_ref, o_ref):
    def clear(k, c):
        o_ref[k] = 0
        return c

    lax.fori_loop(0, 136, clear, 0, unroll=8)

    def put(t, c):
        a = t_ref[0, t]
        b = t_ref[1, t]
        k = t_ref[2, t]
        o_ref[k] = o_ref[k] | (a >> 2) | ((b >> 2) << 8) | (1 << (16 + (a & 3)))
        return c

    lax.fori_loop(0, SLOTS, put, 0, unroll=8)


def table(t):
    return pl.pallas_call(
        table_kernel,
        out_shape=jax.ShapeDtypeStruct((136,), jnp.int32),
        in_specs=[SM],
        out_specs=SM, compiler_params=params(),
        cost_estimate=cost(0, 2**23),
    )(t)


def prep_left(x, ls, at):
    for i in range(4):
        v = x[i * 64 : (i + 1) * 64, :]
        hi = v.astype(BF16)
        ls[at * 4 + i, 0:64, :] = hi
        ls[at * 4 + i, 64:128, :] = (v - hi.astype(F32)).astype(BF16)


def prep_right(x, rs, at):
    lane = lax.broadcasted_iota(jnp.int32, (64, 128), 1)
    for h in range(2):
        for g in range(GROUPS):
            v = x[g * 64 : (g + 1) * 64, h * 128 : (h + 1) * 128]
            hi = v.astype(BF16).astype(F32)
            lo = pltpu.roll(v - hi, 64, 1)
            rs[at * 4 + 2 * h, g * 64 : (g + 1) * 64, :] = jnp.where(lane < 64, hi, lo).astype(BF16)
            rs[at * 4 + 2 * h + 1, g * 64 : (g + 1) * 64, :] = jnp.where(lane < 64, lo, hi).astype(BF16)


def one_slot(word, ls, rs):
    i = word & 255
    j = (word >> 8) & 255
    g = lax.broadcasted_iota(jnp.int32, (1, 256), 1) // 64
    used = (((word >> 16) >> g) & 1).astype(F32).astype(BF16)
    p = jnp.dot(ls[i] * used, rs[j], preferred_element_type=F32)
    return p[:64] + p[64:]


def two_slots(k, tab, ls, rs):
    xa = one_slot(tab[k], ls, rs)
    xb = one_slot(tab[k + 1], ls, rs)
    lane = lax.broadcasted_iota(jnp.int32, (64, 128), 1)
    u = jnp.where(lane < 64, xa, xb)
    v = jnp.where(lane < 64, xb, xa)
    return u + pltpu.roll(v, 64, 1)


def share_into(tab, first, o_ref, at, count, ls, rs):
    def step(p, c):
        for q in range(4):
            n = p * 4 + q
            o_ref[pl.ds(at + n * 64, 64), :] = two_slots(first + 2 * n, tab, ls, rs)
        return c

    lax.fori_loop(0, count // 4, step, 0)


def first_kernel(where, tab, l0, lz1, lz2, la0, lb0, lc0, la, lb, lc, r4, s4, p3, m3, f0, f1, ls, rs):
    me, col, row = where[0], where[1], where[2]
    z, x = col >> 2, col & 3

    def at(dz, dx):
        return lax.rem(z + 3 - dz, 3) * 4 + ((x + 4 - dx) & 3)

    prep_left(l0, ls, at(0, 0))
    prep_left(lz1, ls, at(1, 0))
    prep_left(lz2, ls, at(2, 0))
    prep_left(la0, ls, at(0, 1))
    prep_left(lb0, ls, at(0, 3))
    prep_left(lc0, ls, at(0, 2))
    for h in range(2):
        prep_left(la.at[pl.ds(h * 256, 256)], ls, at(1 + h, 1))
        prep_left(lb.at[pl.ds(h * 256, 256)], ls, at(1 + h, 3))
        prep_left(lc.at[pl.ds(h * 256, 256)], ls, at(1 + h, 2))
    zl, core = row >> 1, row & 1
    for k in range(4):
        prep_right(r4.at[pl.ds(k * 256, 256)], rs, ((zl + 4 - k) & 3) * 2 + core)
        prep_right(s4.at[pl.ds(k * 256, 256)], rs, ((zl + 4 - k) & 3) * 2 + 1 - core)

    def share(k):
        return ((me + 8 + k) & 7) * SHARE

    share_into(tab, share(3), p3, 0, 8, ls, rs)
    share_into(tab, share(1), p3, 512, 8, ls, rs)
    share_into(tab, share(-3), m3, 0, 8, ls, rs)
    share_into(tab, share(-1), m3, 512, 8, ls, rs)
    share_into(tab, share(4), f0, 0, 4, ls, rs)
    share_into(tab, share(4) + 8, f1, 0, 4, ls, rs)


def first(where, tab, parts):
    two = jax.ShapeDtypeStruct((1024, 128), F32)
    half = jax.ShapeDtypeStruct((256, 128), F32)
    return pl.pallas_call(
        first_kernel,
        out_shape=(
            two,
            two,
            half,
            half,
            jax.ShapeDtypeStruct((48, 128, 256), BF16),
            jax.ShapeDtypeStruct((32, 256, 128), BF16),
        ),
        in_specs=[SM, SM] + [VM] * len(parts),
        out_specs=(VM,) * 6,
        compiler_params=params(),
        cost_estimate=cost(2**30, 2**24),
    )(where, tab, *parts)


def second_kernel(where, tab, ls, rs, up, dn, own):
    me = where[0]

    def share(k):
        return ((me + 8 + k) & 7) * SHARE

    share_into(tab, share(2), up, 0, 8, ls, rs)
    share_into(tab, share(-2), dn, 0, 8, ls, rs)
    share_into(tab, share(0), own, 0, 8, ls, rs)


def second(where, tab, ls, rs):
    o = jax.ShapeDtypeStruct((512, 128), F32)
    return pl.pallas_call(
        second_kernel,
        out_shape=(o, o, o),
        in_specs=[SM, SM, VM, VM],
        out_specs=(VM, VM, VM),
        compiler_params=params(),
        cost_estimate=cost(2**29, 2**23),
    )(where, tab, ls, rs)


def middle_kernel(up, dn, q1, q2, q3, q4, u, d):
    u[0:256, :] = up[0:256, :] + q1[0:256, :] + q3[...]
    u[256:512, :] = up[256:512, :] + q1[256:512, :]
    d[0:256, :] = dn[0:256, :] + q2[0:256, :]
    d[256:512, :] = dn[256:512, :] + q2[256:512, :] + q4[...]


def middle(*a):
    o = jax.ShapeDtypeStruct((512, 128), F32)
    return pl.pallas_call(
        middle_kernel, out_shape=(o, o), in_specs=[VM] * 6, compiler_params=params(), out_specs=(VM, VM), cost_estimate=cost(0, 2**21)
    )(*a)


def last_kernel(own, q1, q2, u, d, o_ref):
    for p in range(8):
        s = slice(p * 64, (p + 1) * 64)
        t = slice(512 + p * 64, 512 + (p + 1) * 64)
        v = own[s, :] + q1[t, :] + q2[t, :] + u[s, :] + d[s, :]
        o_ref[2 * p] = v[:, 0:64]
        o_ref[2 * p + 1] = v[:, 64:128]


def last(*a):
    return pl.pallas_call(
        last_kernel,
        out_shape=jax.ShapeDtypeStruct((SHARE, BS, BS), F32),
        in_specs=[VM] * 5, compiler_params=params(),
        out_specs=VM,
        cost_estimate=cost(0, 2**21),
    )(*a)


def along_col(x, dz, dx):
    return lax.ppermute(
        x, "col", [(z * 4 + c, (z + dz) % 3 * 4 + (c + dx) % 4) for z in range(3) for c in range(4)]
    )


def along_row(x, dz, dc):
    return lax.ppermute(
        x, "row", [(z * 2 + c, (z + dz) % 4 * 2 + (c + dc) % 2) for z in range(4) for c in range(2)]
    )


def along_depth(x, k):
    return lax.ppermute(x, "depth", [(i, (i + k) % LAYERS) for i in range(LAYERS)])


def pass_on(a, b):
    h = a.shape[0] // 2
    return jnp.concatenate([along_col(a[:h], 0, 1), along_col(b[h:], 0, -1)])


def per_device(left_blocks, right_blocks, triples):
    me = lax.axis_index("depth")
    where = jnp.stack([me, lax.axis_index("col"), lax.axis_index("row")]).astype(jnp.int32)
    l, r = pack(left_blocks, right_blocks)
    tab = table(triples)
    lz1, lz2 = along_col(l, 1, 0), along_col(l, 2, 0)
    la0, lb0 = along_col(l, 0, 1), along_col(l, 0, -1)
    lc0 = pass_on(la0, lb0)
    lz1, lz2, r = lax.optimization_barrier((lz1, lz2, r))
    l2 = jnp.concatenate([lz1, lz2])
    la, lb = along_col(l2, 0, 1), along_col(l2, 0, -1)
    r4 = jnp.concatenate([r] + [along_row(r, k, 0) for k in (1, 2, 3)])
    la, lb = lax.optimization_barrier((la, lb))
    h = 128
    up_half = along_col(jnp.concatenate([la[:h], la[256 : 256 + h]]), 0, 1)
    dn_half = along_col(jnp.concatenate([lb[h:256], lb[256 + h :]]), 0, -1)
    lc = jnp.concatenate([up_half[:h], dn_half[:h], up_half[h:], dn_half[h:]])
    s4 = along_row(r4, 0, 1)
    p3, m3, f0, f1, ls, rs = first(where, tab, (l, lz1, lz2, la0, lb0, lc0, la, lb, lc, r4, s4))
    q1, q2 = along_depth(p3, 1), along_depth(m3, -1)
    q3, q4 = along_depth(f0, 2), along_depth(f1, -2)
    up, dn, own = second(where, tab, ls, rs)
    u, d = middle(up, dn, q1, q2, q3, q4)
    u, d = along_depth(u, 2), along_depth(d, -2)
    return last(own, q1, q2, u, d)


def solution(mesh):
    placed = (
        P(("row", "col", "depth"), None, None),
        P(("row", "col", "depth"), None, None),
        P(None, ("row", "col", "depth")),
    )
    return jax.shard_map(
        per_device,
        mesh=mesh,
        in_specs=placed,
        out_specs=P(("row", "col", "depth"), None, None),
        check_vma=False,
    )
```

time: 554 us -> 154 us (0.28)
  the two profiles are of different devices: /device:TPU:1 before, /device:TPU:72 now
where the time goes in v1:
time: 154 us; the launch traced here: 153 us
  starting transfers between devices  86.5 us (56%)
  waiting for transfers between devices  48.4 us (31%)
  Pallas kernels  13.7 us (9%)
  local copies, waits for them, and re-layouts  3.7 us (2%)
    ppermute x10, starting transfers between devices, along_col(): lax.ppermute(x, 'col', [(z * 4 + c, (z + dz) % 3 * 4 + (c + dx) % 4) for...  42.8 us
    ppermute x4, starting transfers between devices, along_row(): lax.ppermute(x, 'row', [(z * 2 + c, (z + dz) % 4 * 2 + (c + dc) % 2) for...  22 us
    ppermute x6, starting transfers between devices, along_depth(): lax.ppermute(x, 'depth', [(i, (i + k) % LAYERS) for i in range(LAYERS)])  21.7 us
    ppermute x10, waiting for transfers between devices, along_col(): lax.ppermute(x, 'col', [(z * 4 + c, (z + dz) % 3 * 4 + (c + dx) % 4) for...  21.5 us
    ppermute x6, waiting for transfers between devices, along_depth(): lax.ppermute(x, 'depth', [(i, (i + k) % LAYERS) for i in range(LAYERS)])  19.5 us
    ppermute x4, waiting for transfers between devices, along_row(): lax.ppermute(x, 'row', [(z * 2 + c, (z + dz) % 4 * 2 + (c + dc) % 2) for...  7.33 us
    pallas_call x1, Pallas kernels, table(): pl.pallas_call(table_kernel, out_shape=jax.ShapeDtypeStruct((136,), jnp.i...  4.94 us
    pallas_call x1, Pallas kernels, first(): pl.pallas_call(first_kernel, out_shape=(two, two, half, half, jax.ShapeDt...  4.79 us
  transfers between devices with their start and end apart: 20, of which 7 were waited for; matrix products, arithmetic and copies ran while one was open for 1% of the time, Pallas kernels for 5%

profile of v1, /device:TPU:72, one launch (start us, length us, event | category | flops | bytes accessed | tf_op | source)
XLA Modules:
  0.0 152.9 jit_solution(754429814774094662)
XLA Ops:
  0.0 1.0 copy-done
  1.0 1.0 copy-done.1
  2.1 0.2 shard_map.38
  2.3 13.7 %collective-permute-start.1 = (f32[256,256]{1,0:T(8,128)S(1)}, f32[256,256]{1,0:T(8,128)S(1)}, u32[]{:S(2)}, u32[]{:S(2)}) collective-permute-start(f32[256,256]{1,0:T(8,128)S(1)} %get-tuple-element.23.l0), channel_id=1, source_target_pairs={{0,64},{8,72},{16,80},{24,88},{32,0},{40,8},{48,16},{56,24},{64,32... | collective-permute-start | bytes 786440 | tf_op jit(solution)/shard_map/ppermute | solution.py:232
  16.0 1.9 %collective-permute-start = (f32[256,256]{1,0:T(8,128)S(1)}, f32[256,256]{1,0:T(8,128)S(1)}, u32[]{:S(2)}, u32[]{:S(2)}) collective-permute-start(f32[256,256]{1,0:T(8,128)S(1)} %get-tuple-element.23.l0), channel_id=1, source_target_pairs={{0,32},{8,40},{16,48},{24,56},{32,64},{40,72},{48,80},{56,88},{64,... | collective-permute-start | bytes 786440 | tf_op jit(solution)/shard_map/ppermute | solution.py:232
  17.9 4.7 %collective-permute-start.3 = (f32[256,256]{1,0:T(8,128)S(1)}, f32[256,256]{1,0:T(8,128)S(1)}, u32[]{:S(2)}, u32[]{:S(2)}) collective-permute-start(f32[256,256]{1,0:T(8,128)S(1)} %get-tuple-element.23.l0), channel_id=1, source_target_pairs={{0,24},{8,0},{16,8},{24,16},{32,56},{40,32},{48,40},{56,48},{64,88... | collective-permute-start | bytes 786440 | tf_op jit(solution)/shard_map/ppermute | solution.py:232
  22.6 1.9 %collective-permute-start.2 = (f32[256,256]{1,0:T(8,128)S(1)}, f32[256,256]{1,0:T(8,128)S(1)}, u32[]{:S(2)}, u32[]{:S(2)}) collective-permute-start(f32[256,256]{1,0:T(8,128)S(1)} %get-tuple-element.23.l0), channel_id=1, source_target_pairs={{0,8},{8,16},{16,24},{24,0},{32,40},{40,48},{48,56},{56,32},{64,72... | collective-permute-start | bytes 786440 | tf_op jit(solution)/shard_map/ppermute | solution.py:232
  24.5 12.0 %collective-permute-done.1.lz2 = f32[256,256]{1,0:T(8,128)S(1)} collective-permute-done((f32[256,256]{1,0:T(8,128)S(1)}, f32[256,256]{1,0:T(8,128)S(1)}, u32[]{:S(2)}, u32[]{:S(2)}) %collective-permute-start.1) | collective-permute-done | bytes 262176 | tf_op jit(solution)/shard_map/ppermute | solution.py:232
  36.5 0.0 collective-permute-done.lz1
  36.5 7.8 %collective-permute-start.10 = (f32[256,256]{1,0:T(8,128)S(1)}, f32[256,256]{1,0:T(8,128)S(1)}, u32[]{:S(2)}, u32[]{:S(2)}) collective-permute-start(f32[256,256]{1,0:T(8,128)S(1)} %get-tuple-element.29), channel_id=1, source_target_pairs={{0,192},{96,288},{192,384},{288,480},{384,576},{480,672},{576,0},{... | collective-permute-start | bytes 786440 | tf_op jit(solution)/shard_map/ppermute | solution.py:238
  44.2 0.7 constant_dynamic-update-slice_fusion.1
  45.0 0.7 constant_dynamic-update-slice_fusion
  45.7 4.7 %collective-permute-start.7 = (f32[512,256]{1,0:T(8,128)}, f32[512,256]{1,0:T(8,128)S(1)}, u32[]{:S(2)}, u32[]{:S(2)}) collective-permute-start(f32[512,256]{1,0:T(8,128)} %constant_dynamic-update-slice_fusion), channel_id=1, source_target_pairs={{0,24},{8,0},{16,8},{24,16},{32,56},{40,32},{48,40},{56,48},{64,88... | collective-permute-start | bytes 1572872 | tf_op jit(solution)/shard_map/ppermute | solution.py:232
  50.4 1.9 %collective-permute-start.6 = (f32[512,256]{1,0:T(8,128)}, f32[512,256]{1,0:T(8,128)S(1)}, u32[]{:S(2)}, u32[]{:S(2)}) collective-permute-start(f32[512,256]{1,0:T(8,128)} %constant_dynamic-update-slice_fusion), channel_id=1, source_target_pairs={{0,8},{8,16},{16,24},{24,0},{32,40},{40,48},{48,56},{56,32},{64,72... | collective-permute-start | bytes 1572872 | tf_op jit(solution)/shard_map/ppermute | solution.py:232
  52.3 8.9 %collective-permute-start.11 = (f32[256,256]{1,0:T(8,128)S(1)}, f32[256,256]{1,0:T(8,128)S(1)}, u32[]{:S(2)}, u32[]{:S(2)}) collective-permute-start(f32[256,256]{1,0:T(8,128)S(1)} %get-tuple-element.29), channel_id=1, source_target_pairs={{0,384},{96,480},{192,576},{288,672},{384,0},{480,96},{576,192},{6... | collective-permute-start | bytes 786440 | tf_op jit(solution)/shard_map/ppermute | solution.py:238
  61.3 3.3 %collective-permute-start.12 = (f32[256,256]{1,0:T(8,128)S(1)}, f32[256,256]{1,0:T(8,128)S(1)}, u32[]{:S(2)}, u32[]{:S(2)}) collective-permute-start(f32[256,256]{1,0:T(8,128)S(1)} %get-tuple-element.29), channel_id=1, source_target_pairs={{0,576},{96,672},{192,0},{288,96},{384,192},{480,288},{576,384},{6... | collective-permute-start | bytes 786440 | tf_op jit(solution)/shard_map/ppermute | solution.py:238
  64.7 0.0 collective-permute-done.10
  64.7 5.1 %collective-permute-start.5 = (f32[128,256]{1,0:T(8,128)S(1)}, f32[128,256]{1,0:T(8,128)S(1)}, u32[]{:S(2)}, u32[]{:S(2)}) collective-permute-start(f32[128,256]{1,0:T(8,128)S(1)} %slice.41), channel_id=1, source_target_pairs={{0,24},{8,0},{16,8},{24,16},{32,56},{40,32},{48,40},{56,48},{64,88... | collective-permute-start | bytes 393224 | tf_op jit(solution)/shard_map/ppermute | solution.py:232
  69.8 7.3 %collective-permute-done.11 = f32[256,256]{1,0:T(8,128)S(1)} collective-permute-done((f32[256,256]{1,0:T(8,128)S(1)}, f32[256,256]{1,0:T(8,128)S(1)}, u32[]{:S(2)}, u32[]{:S(2)}) %collective-permute-start.11) | collective-permute-done | bytes 262176 | tf_op jit(solution)/shard_map/ppermute | solution.py:238
  77.2 2.4 %collective-permute-start.4 = (f32[128,256]{1,0:T(8,128)S(1)}, f32[128,256]{1,0:T(8,128)S(1)}, u32[]{:S(2)}, u32[]{:S(2)}) collective-permute-start(f32[128,256]{1,0:T(8,128)S(1)} %slice.40), channel_id=1, source_target_pairs={{0,8},{8,16},{16,24},{24,0},{32,40},{40,48},{48,56},{56,32},{64,72... | collective-permute-start | bytes 393224 | tf_op jit(solution)/shard_map/ppermute | solution.py:232
  79.6 0.0 collective-permute-done.12
  79.6 1.9 %collective-permute-start.13 = (f32[1024,256]{1,0:T(8,128)S(1)}, f32[1024,256]{1,0:T(8,128)S(1)}, u32[]{:S(2)}, u32[]{:S(2)}) collective-permute-start(f32[1024,256]{1,0:T(8,128)S(1)} %constant_dynamic-update-slice_fusion.2.r4), channel_id=1, source_target_pairs={{0,96},{96,0},{192,288},{288,192},{384,480},{480,384},{576,672},{6... | collective-permute-start | bytes 3145736 | tf_op jit(solution)/shard_map/ppermute | solution.py:238
  81.5 0.0 collective-permute-done.6.la
  81.6 4.7 %collective-permute-start.9 = (f32[256,256]{1,0:T(8,128)S(1)}, f32[256,256]{1,0:T(8,128)S(1)}, u32[]{:S(2)}, u32[]{:S(2)}) collective-permute-start(f32[256,256]{1,0:T(8,128)S(1)} %pad_maximum_fusion.3), channel_id=1, source_target_pairs={{0,24},{8,0},{16,8},{24,16},{32,56},{40,32},{48,40},{56,48},{64,88... | collective-permute-start | bytes 786440 | tf_op jit(solution)/shard_map/ppermute | solution.py:232
  86.3 0.1 pad_add_fusion.where
  86.4 4.9 %shard_map.37.tab = s32[136]{0:T(256)S(1)} custom-call(s32[3,512]{1,0:T(4,128)S(1)} %copy-done.2), custom_call_target="tpu_custom_call" | custom-call | bytes 8388608 | tf_op jit(solution)/shard_map/pallas_call | solution.py:66
  91.4 1.9 %collective-permute-start.8 = (f32[256,256]{1,0:T(8,128)S(1)}, f32[256,256]{1,0:T(8,128)S(1)}, u32[]{:S(2)}, u32[]{:S(2)}) collective-permute-start(f32[256,256]{1,0:T(8,128)S(1)} %pad_maximum_fusion.2), channel_id=1, source_target_pairs={{0,8},{8,16},{16,24},{24,0},{32,40},{40,48},{48,56},{56,32},{64,72... | collective-permute-start | bytes 786440 | tf_op jit(solution)/shard_map/ppermute | solution.py:232
  93.3 0.0 collective-permute-done.5
  93.3 0.0 collective-permute-done.4
  93.3 0.0 collective-permute-done.9
  93.4 9.5 %collective-permute-done.8 = f32[256,256]{1,0:T(8,128)S(1)} collective-permute-done((f32[256,256]{1,0:T(8,128)S(1)}, f32[256,256]{1,0:T(8,128)S(1)}, u32[]{:S(2)}, u32[]{:S(2)}) %collective-permute-start.8) | collective-permute-done | bytes 262176 | tf_op jit(solution)/shard_map/ppermute | solution.py:232
  103.0 0.0 collective-permute-done.13.s4
  103.0 4.8 %shard_map.39 = (f32[1024,128]{1,0:T(8,128)S(1)}, f32[1024,128]{1,0:T(8,128)S(1)}, f32[256,128]{1,0:T(8,128)S(1)}, f32[256,128]{1,0:T(8,128)S(1)}, bf16[48,128,2...) custom-call(s32[3]{0:T(128)S(1)} %pad_add_fusion.where, s32[136]{0:T(256)S(1)} %shard_map.37.tab, ...), custom_call_target="tpu_custom_call" | custom-call | flops 1073741824 | bytes 16777216 | tf_op jit(solution)/shard_map/pallas_call | solution.py:158
  107.8 3.5 %collective-permute-start.14 = (f32[1024,128]{1,0:T(8,128)S(1)}, f32[1024,128]{1,0:T(8,128)S(1)}, u32[]{:S(2)}, u32[]{:S(2)}) collective-permute-start(f32[1024,128]{1,0:T(8,128)S(1)} %get-tuple-element.33), channel_id=1, source_target_pairs={{0,1},{1,2},{2,3},{3,4},{4,5},{5,6},{6,7},{7,0},{8,9},{9,10},{10,1... | collective-permute-start | bytes 1572872 | tf_op jit(solution)/shard_map/ppermute | solution.py:244
  111.3 2.4 %collective-permute-start.15 = (f32[1024,128]{1,0:T(8,128)S(1)}, f32[1024,128]{1,0:T(8,128)S(1)}, u32[]{:S(2)}, u32[]{:S(2)}) collective-permute-start(f32[1024,128]{1,0:T(8,128)S(1)} %get-tuple-element.34), channel_id=1, source_target_pairs={{0,7},{1,0},{2,1},{3,2},{4,3},{5,4},{6,5},{7,6},{8,15},{9,8},{10,9... | collective-permute-start | bytes 1572872 | tf_op jit(solution)/shard_map/ppermute | solution.py:244
  113.6 5.3 %collective-permute-start.16 = (f32[256,128]{1,0:T(8,128)S(1)}, f32[256,128]{1,0:T(8,128)S(1)}, u32[]{:S(2)}, u32[]{:S(2)}) collective-permute-start(f32[256,128]{1,0:T(8,128)S(1)} %get-tuple-element.37), channel_id=1, source_target_pairs={{0,2},{1,3},{2,4},{3,5},{4,6},{5,7},{6,0},{7,1},{8,10},{9,11},{10,... | collective-permute-start | bytes 393224 | tf_op jit(solution)/shard_map/ppermute | solution.py:244
  118.9 2.7 %collective-permute-start.17 = (f32[256,128]{1,0:T(8,128)S(1)}, f32[256,128]{1,0:T(8,128)S(1)}, u32[]{:S(2)}, u32[]{:S(2)}) collective-permute-start(f32[256,128]{1,0:T(8,128)S(1)} %get-tuple-element.38), channel_id=1, source_target_pairs={{0,6},{1,7},{2,0},{3,1},{4,2},{5,3},{6,4},{7,5},{8,14},{9,15},{10,... | collective-permute-start | bytes 393224 | tf_op jit(solution)/shard_map/ppermute | solution.py:244
  121.6 2.7 %shard_map.40 = (f32[512,128]{1,0:T(8,128)S(1)}, f32[512,128]{1,0:T(8,128)S(1)}, f32[512,128]{1,0:T(8,128)S(1)}) custom-call(s32[3]{0:T(128)S(1)} %pad_add_fusion.where, s32[136]{0:T(256)S(1)} %shard_map.37.tab, bf16[48,128,256]{2,1,0:T(8,128)(2,1)S(1)} %get-tuple-element.30.ls, bf16[32,256,128]{2,1,0:T(8,128)(2,1)S(1)} %get-tuple-element.31.rs), custom_call_target="tpu_custom_call" | custom-call | flops 536870912 | bytes 8388608 | tf_op jit(solution)/shard_map/pallas_call | solution.py:188
  124.3 5.8 %collective-permute-done.16.q3 = f32[256,128]{1,0:T(8,128)S(1)} collective-permute-done((f32[256,128]{1,0:T(8,128)S(1)}, f32[256,128]{1,0:T(8,128)S(1)}, u32[]{:S(2)}, u32[]{:S(2)}) %collective-permute-start.16) | collective-permute-done | bytes 131104 | tf_op jit(solution)/shard_map/ppermute | solution.py:244
  130.1 1.8 %collective-permute-done.17.q4 = f32[256,128]{1,0:T(8,128)S(1)} collective-permute-done((f32[256,128]{1,0:T(8,128)S(1)}, f32[256,128]{1,0:T(8,128)S(1)}, u32[]{:S(2)}, u32[]{:S(2)}) %collective-permute-start.17) | collective-permute-done | bytes 131104 | tf_op jit(solution)/shard_map/ppermute | solution.py:244
  131.9 0.0 collective-permute-done.14.q1
  131.9 0.0 collective-permute-done.15.q2
  131.9 0.1 shard_map.41
  132.0 5.3 %collective-permute-start.18 = (f32[512,128]{1,0:T(8,128)S(1)}, f32[512,128]{1,0:T(8,128)S(1)}, u32[]{:S(2)}, u32[]{:S(2)}) collective-permute-start(f32[512,128]{1,0:T(8,128)S(1)} %get-tuple-element.39), channel_id=1, source_target_pairs={{0,2},{1,3},{2,4},{3,5},{4,6},{5,7},{6,0},{7,1},{8,10},{9,11},{10,... | collective-permute-start | bytes 786440 | tf_op jit(solution)/shard_map/ppermute | solution.py:244
  137.3 2.6 %collective-permute-start.19 = (f32[512,128]{1,0:T(8,128)S(1)}, f32[512,128]{1,0:T(8,128)S(1)}, u32[]{:S(2)}, u32[]{:S(2)}) collective-permute-start(f32[512,128]{1,0:T(8,128)S(1)} %get-tuple-element.40), channel_id=1, source_target_pairs={{0,6},{1,7},{2,0},{3,1},{4,2},{5,3},{6,4},{7,5},{8,14},{9,15},{10,... | collective-permute-start | bytes 786440 | tf_op jit(solution)/shard_map/ppermute | solution.py:244
  140.0 3.1 %collective-permute-done.18.u = f32[512,128]{1,0:T(8,128)S(1)} collective-permute-done((f32[512,128]{1,0:T(8,128)S(1)}, f32[512,128]{1,0:T(8,128)S(1)}, u32[]{:S(2)}, u32[]{:S(2)}) %collective-permute-start.18) | collective-permute-done | bytes 262176 | tf_op jit(solution)/shard_map/ppermute | solution.py:244
  143.1 8.8 %collective-permute-done.19.d = f32[512,128]{1,0:T(8,128)S(1)} collective-permute-done((f32[512,128]{1,0:T(8,128)S(1)}, f32[512,128]{1,0:T(8,128)S(1)}, u32[]{:S(2)}, u32[]{:S(2)}) %collective-permute-start.19) | collective-permute-done | bytes 262176 | tf_op jit(solution)/shard_map/ppermute | solution.py:244
  151.9 1.0 shard_map.42
  (20 shorter events, 0.3 us)
Async XLA Ops:
  0.0 1.0 copy-start
  1.0 1.0 copy-start.1
  2.1 84.3 %copy-start.2 = (s32[3,512]{1,0:T(4,128)S(1)}, s32[3,512]{1,0:T(4,128)}, u32[]{:S(2)}) copy-start(s32[3,512]{1,0:T(4,128)} %t_ref.1) | copy-start | bytes 18436
  2.3 34.2 %collective-permute-start.1 = (f32[256,256]{1,0:T(8,128)S(1)}, f32[256,256]{1,0:T(8,128)S(1)}, u32[]{:S(2)}, u32[]{:S(2)}) collective-permute-start(f32[256,256]{1,0:T(8,128)S(1)} %get-tuple-element.23.l0), channel_id=1, source_target_pairs={{0,64},{8,72},{16,80},{24,88},{32,0},{40,8},{48,16},{56,24},{64,32... | collective-permute-start | bytes 786440 | tf_op jit(solution)/shard_map/ppermute | solution.py:232
  16.0 20.5 %collective-permute-start = (f32[256,256]{1,0:T(8,128)S(1)}, f32[256,256]{1,0:T(8,128)S(1)}, u32[]{:S(2)}, u32[]{:S(2)}) collective-permute-start(f32[256,256]{1,0:T(8,128)S(1)} %get-tuple-element.23.l0), channel_id=1, source_target_pairs={{0,32},{8,40},{16,48},{24,56},{32,64},{40,72},{48,80},{56,88},{64,... | collective-permute-start | bytes 786440 | tf_op jit(solution)/shard_map/ppermute | solution.py:232
  17.9 34.4 %collective-permute-start.3 = (f32[256,256]{1,0:T(8,128)S(1)}, f32[256,256]{1,0:T(8,128)S(1)}, u32[]{:S(2)}, u32[]{:S(2)}) collective-permute-start(f32[256,256]{1,0:T(8,128)S(1)} %get-tuple-element.23.l0), channel_id=1, source_target_pairs={{0,24},{8,0},{16,8},{24,16},{32,56},{40,32},{48,40},{56,48},{64,88... | collective-permute-start | bytes 786440 | tf_op jit(solution)/shard_map/ppermute | solution.py:232
  22.6 38.7 %collective-permute-start.2 = (f32[256,256]{1,0:T(8,128)S(1)}, f32[256,256]{1,0:T(8,128)S(1)}, u32[]{:S(2)}, u32[]{:S(2)}) collective-permute-start(f32[256,256]{1,0:T(8,128)S(1)} %get-tuple-element.23.l0), channel_id=1, source_target_pairs={{0,8},{8,16},{16,24},{24,0},{32,40},{40,48},{48,56},{56,32},{64,72... | collective-permute-start | bytes 786440 | tf_op jit(solution)/shard_map/ppermute | solution.py:232
  36.5 28.2 %collective-permute-start.10 = (f32[256,256]{1,0:T(8,128)S(1)}, f32[256,256]{1,0:T(8,128)S(1)}, u32[]{:S(2)}, u32[]{:S(2)}) collective-permute-start(f32[256,256]{1,0:T(8,128)S(1)} %get-tuple-element.29), channel_id=1, source_target_pairs={{0,192},{96,288},{192,384},{288,480},{384,576},{480,672},{576,0},{... | collective-permute-start | bytes 786440 | tf_op jit(solution)/shard_map/ppermute | solution.py:238
  45.7 35.8 %collective-permute-start.7 = (f32[512,256]{1,0:T(8,128)}, f32[512,256]{1,0:T(8,128)S(1)}, u32[]{:S(2)}, u32[]{:S(2)}) collective-permute-start(f32[512,256]{1,0:T(8,128)} %constant_dynamic-update-slice_fusion), channel_id=1, source_target_pairs={{0,24},{8,0},{16,8},{24,16},{32,56},{40,32},{48,40},{56,48},{64,88... | collective-permute-start | bytes 1572872 | tf_op jit(solution)/shard_map/ppermute | solution.py:232
  50.4 31.2 %collective-permute-start.6 = (f32[512,256]{1,0:T(8,128)}, f32[512,256]{1,0:T(8,128)S(1)}, u32[]{:S(2)}, u32[]{:S(2)}) collective-permute-start(f32[512,256]{1,0:T(8,128)} %constant_dynamic-update-slice_fusion), channel_id=1, source_target_pairs={{0,8},{8,16},{16,24},{24,0},{32,40},{40,48},{48,56},{56,32},{64,72... | collective-permute-start | bytes 1572872 | tf_op jit(solution)/shard_map/ppermute | solution.py:232
  52.3 24.9 %collective-permute-start.11 = (f32[256,256]{1,0:T(8,128)S(1)}, f32[256,256]{1,0:T(8,128)S(1)}, u32[]{:S(2)}, u32[]{:S(2)}) collective-permute-start(f32[256,256]{1,0:T(8,128)S(1)} %get-tuple-element.29), channel_id=1, source_target_pairs={{0,384},{96,480},{192,576},{288,672},{384,0},{480,96},{576,192},{6... | collective-permute-start | bytes 786440 | tf_op jit(solution)/shard_map/ppermute | solution.py:238
  61.3 18.3 %collective-permute-start.12 = (f32[256,256]{1,0:T(8,128)S(1)}, f32[256,256]{1,0:T(8,128)S(1)}, u32[]{:S(2)}, u32[]{:S(2)}) collective-permute-start(f32[256,256]{1,0:T(8,128)S(1)} %get-tuple-element.29), channel_id=1, source_target_pairs={{0,576},{96,672},{192,0},{288,96},{384,192},{480,288},{576,384},{6... | collective-permute-start | bytes 786440 | tf_op jit(solution)/shard_map/ppermute | solution.py:238
  64.7 28.6 %collective-permute-start.5 = (f32[128,256]{1,0:T(8,128)S(1)}, f32[128,256]{1,0:T(8,128)S(1)}, u32[]{:S(2)}, u32[]{:S(2)}) collective-permute-start(f32[128,256]{1,0:T(8,128)S(1)} %slice.41), channel_id=1, source_target_pairs={{0,24},{8,0},{16,8},{24,16},{32,56},{40,32},{48,40},{56,48},{64,88... | collective-permute-start | bytes 393224 | tf_op jit(solution)/shard_map/ppermute | solution.py:232
  77.2 16.1 %collective-permute-start.4 = (f32[128,256]{1,0:T(8,128)S(1)}, f32[128,256]{1,0:T(8,128)S(1)}, u32[]{:S(2)}, u32[]{:S(2)}) collective-permute-start(f32[128,256]{1,0:T(8,128)S(1)} %slice.40), channel_id=1, source_target_pairs={{0,8},{8,16},{16,24},{24,0},{32,40},{40,48},{48,56},{56,32},{64,72... | collective-permute-start | bytes 393224 | tf_op jit(solution)/shard_map/ppermute | solution.py:232
  79.6 23.4 %collective-permute-start.13 = (f32[1024,256]{1,0:T(8,128)S(1)}, f32[1024,256]{1,0:T(8,128)S(1)}, u32[]{:S(2)}, u32[]{:S(2)}) collective-permute-start(f32[1024,256]{1,0:T(8,128)S(1)} %constant_dynamic-update-slice_fusion.2.r4), channel_id=1, source_target_pairs={{0,96},{96,0},{192,288},{288,192},{384,480},{480,384},{576,672},{6... | collective-permute-start | bytes 3145736 | tf_op jit(solution)/shard_map/ppermute | solution.py:238
  81.6 11.7 %collective-permute-start.9 = (f32[256,256]{1,0:T(8,128)S(1)}, f32[256,256]{1,0:T(8,128)S(1)}, u32[]{:S(2)}, u32[]{:S(2)}) collective-permute-start(f32[256,256]{1,0:T(8,128)S(1)} %pad_maximum_fusion.3), channel_id=1, source_target_pairs={{0,24},{8,0},{16,8},{24,16},{32,56},{40,32},{48,40},{56,48},{64,88... | collective-permute-start | bytes 786440 | tf_op jit(solution)/shard_map/ppermute | solution.py:232
  91.4 11.5 %collective-permute-start.8 = (f32[256,256]{1,0:T(8,128)S(1)}, f32[256,256]{1,0:T(8,128)S(1)}, u32[]{:S(2)}, u32[]{:S(2)}) collective-permute-start(f32[256,256]{1,0:T(8,128)S(1)} %pad_maximum_fusion.2), channel_id=1, source_target_pairs={{0,8},{8,16},{16,24},{24,0},{32,40},{40,48},{48,56},{56,32},{64,72... | collective-permute-start | bytes 786440 | tf_op jit(solution)/shard_map/ppermute | solution.py:232
  107.8 24.1 %collective-permute-start.14 = (f32[1024,128]{1,0:T(8,128)S(1)}, f32[1024,128]{1,0:T(8,128)S(1)}, u32[]{:S(2)}, u32[]{:S(2)}) collective-permute-start(f32[1024,128]{1,0:T(8,128)S(1)} %get-tuple-element.33), channel_id=1, source_target_pairs={{0,1},{1,2},{2,3},{3,4},{4,5},{5,6},{6,7},{7,0},{8,9},{9,10},{10,1... | collective-permute-start | bytes 1572872 | tf_op jit(solution)/shard_map/ppermute | solution.py:244
  111.3 20.7 %collective-permute-start.15 = (f32[1024,128]{1,0:T(8,128)S(1)}, f32[1024,128]{1,0:T(8,128)S(1)}, u32[]{:S(2)}, u32[]{:S(2)}) collective-permute-start(f32[1024,128]{1,0:T(8,128)S(1)} %get-tuple-element.34), channel_id=1, source_target_pairs={{0,7},{1,0},{2,1},{3,2},{4,3},{5,4},{6,5},{7,6},{8,15},{9,8},{10,9... | collective-permute-start | bytes 1572872 | tf_op jit(solution)/shard_map/ppermute | solution.py:244
  113.6 16.5 %collective-permute-start.16 = (f32[256,128]{1,0:T(8,128)S(1)}, f32[256,128]{1,0:T(8,128)S(1)}, u32[]{:S(2)}, u32[]{:S(2)}) collective-permute-start(f32[256,128]{1,0:T(8,128)S(1)} %get-tuple-element.37), channel_id=1, source_target_pairs={{0,2},{1,3},{2,4},{3,5},{4,6},{5,7},{6,0},{7,1},{8,10},{9,11},{10,... | collective-permute-start | bytes 393224 | tf_op jit(solution)/shard_map/ppermute | solution.py:244
  118.9 13.0 %collective-permute-start.17 = (f32[256,128]{1,0:T(8,128)S(1)}, f32[256,128]{1,0:T(8,128)S(1)}, u32[]{:S(2)}, u32[]{:S(2)}) collective-permute-start(f32[256,128]{1,0:T(8,128)S(1)} %get-tuple-element.38), channel_id=1, source_target_pairs={{0,6},{1,7},{2,0},{3,1},{4,2},{5,3},{6,4},{7,5},{8,14},{9,15},{10,... | collective-permute-start | bytes 393224 | tf_op jit(solution)/shard_map/ppermute | solution.py:244
  132.0 11.1 %collective-permute-start.18 = (f32[512,128]{1,0:T(8,128)S(1)}, f32[512,128]{1,0:T(8,128)S(1)}, u32[]{:S(2)}, u32[]{:S(2)}) collective-permute-start(f32[512,128]{1,0:T(8,128)S(1)} %get-tuple-element.39), channel_id=1, source_target_pairs={{0,2},{1,3},{2,4},{3,5},{4,6},{5,7},{6,0},{7,1},{8,10},{9,11},{10,... | collective-permute-start | bytes 786440 | tf_op jit(solution)/shard_map/ppermute | solution.py:244
  137.3 14.6 %collective-permute-start.19 = (f32[512,128]{1,0:T(8,128)S(1)}, f32[512,128]{1,0:T(8,128)S(1)}, u32[]{:S(2)}, u32[]{:S(2)}) collective-permute-start(f32[512,128]{1,0:T(8,128)S(1)} %get-tuple-element.40), channel_id=1, source_target_pairs={{0,6},{1,7},{2,0},{3,1},{4,2},{5,3},{6,4},{7,5},{8,14},{9,15},{10,... | collective-permute-start | bytes 786440 | tf_op jit(solution)/shard_map/ppermute | solution.py:244

commit v2 on v1

v2 whole, which is shorter than its diff:
```python
import jax
import jax.numpy as jnp
from jax import lax
from jax.experimental import pallas as pl
from jax.experimental.pallas import tpu as pltpu
from jax.sharding import PartitionSpec as P

BS = 64
GROUPS = 4
SLOTS = 512
PC = 128
LAYERS = 8
SHARE = PC // LAYERS
VM = pl.BlockSpec(memory_space=pltpu.VMEM)
SM = pl.BlockSpec(memory_space=pltpu.SMEM)
F32 = jnp.float32
BF16 = jnp.bfloat16


def params():
    return pltpu.CompilerParams(vmem_limit_bytes=16 * 2**20)


def cost(flops, nbytes):
    return pl.CostEstimate(flops=flops, bytes_accessed=nbytes, transcendentals=0)


def pack_left_kernel(l_ref, three_ref, one_ref):
    for i in range(4):
        for h in range(2):
            v = jnp.concatenate([l_ref[4 * i + 2 * h], l_ref[4 * i + 2 * h + 1]], axis=1)
            at = (slice(i * 64, (i + 1) * 64), slice(h * 128, (h + 1) * 128))
            for c in range(3):
                three_ref[(c,) + at] = v
            one_ref[at] = v


def pack_left(l):
    return pl.pallas_call(
        pack_left_kernel,
        out_shape=(jax.ShapeDtypeStruct((3, 256, 256), F32), jax.ShapeDtypeStruct((256, 256), F32)),
        in_specs=[VM],
        out_specs=(VM, VM),
        compiler_params=params(),
        cost_estimate=cost(0, 2**21),
    )(l)


def pack_right_kernel(r_ref, o_ref):
    for g in range(GROUPS):
        for h in range(2):
            o_ref[g * 64 : (g + 1) * 64, h * 128 : (h + 1) * 128] = jnp.concatenate(
                [r_ref[8 * h + g], r_ref[8 * h + 4 + g]], axis=1
            )


def pack_right(r):
    return pl.pallas_call(
        pack_right_kernel,
        out_shape=jax.ShapeDtypeStruct((256, 256), F32),
        in_specs=[VM],
        out_specs=VM,
        compiler_params=params(),
        cost_estimate=cost(0, 2**21),
    )(r)


def table_kernel(t_ref, o_ref):
    def clear(k, c):
        o_ref[k] = 0
        return c

    lax.fori_loop(0, 136, clear, 0, unroll=8)

    def put(t, c):
        a = t_ref[0, t]
        b = t_ref[1, t]
        k = t_ref[2, t]
        o_ref[k] = o_ref[k] | (a >> 2) | ((b >> 2) << 8) | (1 << (16 + (a & 3)))
        return c

    lax.fori_loop(0, SLOTS, put, 0, unroll=8)


def table(t):
    return pl.pallas_call(
        table_kernel,
        out_shape=jax.ShapeDtypeStruct((136,), jnp.int32),
        in_specs=[SM],
        out_specs=SM, compiler_params=params(),
        cost_estimate=cost(0, 2**23),
    )(t)


def prep_left(x, ls, at):
    for i in range(4):
        v = x[i * 64 : (i + 1) * 64, :]
        hi = v.astype(BF16)
        ls[at * 4 + i, 0:64, :] = hi
        ls[at * 4 + i, 64:128, :] = (v - hi.astype(F32)).astype(BF16)


def prep_right(x, rs, at):
    lane = lax.broadcasted_iota(jnp.int32, (64, 128), 1)
    for h in range(2):
        for g in range(GROUPS):
            v = x[g * 64 : (g + 1) * 64, h * 128 : (h + 1) * 128]
            hi = v.astype(BF16).astype(F32)
            lo = pltpu.roll(v - hi, 64, 1)
            rs[at * 4 + 2 * h, g * 64 : (g + 1) * 64, :] = jnp.where(lane < 64, hi, lo).astype(BF16)
            rs[at * 4 + 2 * h + 1, g * 64 : (g + 1) * 64, :] = jnp.where(lane < 64, lo, hi).astype(BF16)


def one_slot(word, ls, rs):
    i = word & 255
    j = (word >> 8) & 255
    g = lax.broadcasted_iota(jnp.int32, (1, 256), 1) // 64
    used = (((word >> 16) >> g) & 1).astype(F32).astype(BF16)
    p = jnp.dot(ls[i] * used, rs[j], preferred_element_type=F32)
    return p[:64] + p[64:]


def two_slots(k, tab, ls, rs):
    xa = one_slot(tab[k], ls, rs)
    xb = one_slot(tab[k + 1], ls, rs)
    lane = lax.broadcasted_iota(jnp.int32, (64, 128), 1)
    u = jnp.where(lane < 64, xa, xb)
    v = jnp.where(lane < 64, xb, xa)
    return u + pltpu.roll(v, 64, 1)


def share_into(tab, first, o_ref, at, count, ls, rs):
    def step(p, c):
        for q in range(4):
            n = p * 4 + q
            o_ref[pl.ds(at + n * 64, 64), :] = two_slots(first + 2 * n, tab, ls, rs)
        return c

    lax.fori_loop(0, count // 4, step, 0)


LEFT = jax.ShapeDtypeStruct((48, 128, 256), BF16)
RIGHT = jax.ShapeDtypeStruct((32, 256, 128), BF16)


def split_own_kernel(where, l0, la, lb, lc, ls):
    z, x = where[1] >> 2, where[1] & 3
    for k, ref in enumerate((l0, la, lb, lc)):
        prep_left(ref, ls, z * 4 + ((x + 4 - k) & 3))


def split_own(where, *parts):
    return pl.pallas_call(
        split_own_kernel,
        out_shape=LEFT,
        in_specs=[SM] + [VM] * 4,
        out_specs=VM,
        compiler_params=params(),
        cost_estimate=cost(0, 2**22),
    )(where, *parts)


def spread_kernel(where, zs, o_ref):
    z = where[1] >> 2
    for h in range(2):
        at = lax.rem(z + 1 + h, 3)
        for q in range(4):
            v = zs[at, q * 64 : (q + 1) * 64, :]
            for c in range(4):
                o_ref[c, h * 256 + q * 64 : h * 256 + (q + 1) * 64, :] = v


def spread(where, zs):
    return pl.pallas_call(
        spread_kernel,
        out_shape=jax.ShapeDtypeStruct((4, 512, 256), F32),
        in_specs=[SM, VM],
        out_specs=VM,
        compiler_params=params(),
        cost_estimate=cost(0, 2**21),
    )(where, zs)


def split_others_kernel(where, ls_in, xs, ls):
    z = where[1] >> 2
    for c in range(4):
        for h in range(2):
            prep_left(xs.at[c, pl.ds(h * 256, 256)], ls, lax.rem(z + 1 + h, 3) * 4 + c)


def split_others(where, ls, xs):
    return pl.pallas_call(
        split_others_kernel,
        out_shape=LEFT,
        in_specs=[SM, VM, VM],
        out_specs=VM,
        input_output_aliases={1: 0},
        compiler_params=params(),
        cost_estimate=cost(0, 2**22),
    )(where, ls, xs)


def first_right_kernel(where, *refs):
    r4, rs = refs[:4], refs[4]
    core = where[2] & 1
    for k in range(4):
        prep_right(r4[k], rs, (((where[2] >> 1) + 4 - k) & 3) * 2 + core)


def first_right(where, r4):
    return pl.pallas_call(
        first_right_kernel,
        out_shape=RIGHT,
        in_specs=[SM] + [VM] * 4,
        out_specs=VM,
        compiler_params=params(),
        cost_estimate=cost(0, 2**22),
    )(where, *r4)


def share_of(where, k):
    return ((where[0] + 8 + k) & 7) * SHARE


def last_right_kernel(where, rs_in, s4, rs):
    core = where[2] & 1
    for k in range(4):
        prep_right(s4.at[k], rs, (((where[2] >> 1) + 4 - k) & 3) * 2 + 1 - core)


def last_right(where, rs, s4):
    return pl.pallas_call(
        last_right_kernel,
        out_shape=RIGHT,
        in_specs=[SM, VM, VM],
        out_specs=VM,
        input_output_aliases={1: 0},
        compiler_params=params(),
        cost_estimate=cost(0, 2**22),
    )(where, rs, s4)


def shares(where, tab, ls, rs, offsets, after):
    def kernel(where, tab, ls, rs, after_ref, o_ref):
        for n, k in enumerate(offsets):
            share_into(tab, share_of(where, k), o_ref, n * 512, 8, ls, rs)

    return pl.pallas_call(
        kernel,
        out_shape=jax.ShapeDtypeStruct((512 * len(offsets), 128), F32),
        in_specs=[SM, SM, VM, VM, pl.BlockSpec(memory_space=pl.ANY)],
        out_specs=VM,
        compiler_params=params(),
        cost_estimate=cost(2**27 * len(offsets), 2**20 * len(offsets)),
    )(where, tab, ls, rs, after)


def far_kernel(where, tab, ls, rs, after_ref, f0, f1):
    share_into(tab, share_of(where, 4), f0, 0, 4, ls, rs)
    share_into(tab, share_of(where, 4) + 8, f1, 0, 4, ls, rs)


def far(where, tab, ls, rs, after):
    half = jax.ShapeDtypeStruct((256, 128), F32)
    return pl.pallas_call(
        far_kernel,
        out_shape=(half, half),
        in_specs=[SM, SM, VM, VM, pl.BlockSpec(memory_space=pl.ANY)],
        out_specs=(VM, VM),
        compiler_params=params(),
        cost_estimate=cost(2**27, 2**20),
    )(where, tab, ls, rs, after)


def up_kernel(near, q, half, o_ref):
    o_ref[0:256, :] = near[0:256, :] + q[0:256, :] + half[...]
    o_ref[256:512, :] = near[256:512, :] + q[256:512, :]


def down_kernel(near, q, half, after_ref, o_ref):
    o_ref[0:256, :] = near[512:768, :] + q[0:256, :]
    o_ref[256:512, :] = near[768:1024, :] + q[256:512, :] + half[...]


def merge(kernel, near, q, half, *after, weight):
    return pl.pallas_call(
        kernel,
        out_shape=jax.ShapeDtypeStruct((512, 128), F32),
        in_specs=[VM] * 3 + [pl.BlockSpec(memory_space=pl.ANY)] * len(after),
        out_specs=VM,
        compiler_params=params(),
        cost_estimate=cost(0, weight),
    )(near, q, half, *after)


def sum_kernel(near, q1, q2, u, o_ref):
    o_ref[...] = near[1024:1536, :] + q1[512:1024, :] + q2[512:1024, :] + u[...]


def partial_sum(*a):
    return pl.pallas_call(
        sum_kernel,
        out_shape=jax.ShapeDtypeStruct((512, 128), F32),
        in_specs=[VM] * 4,
        out_specs=VM,
        compiler_params=params(),
        cost_estimate=cost(0, 2**21),
    )(*a)


def last_kernel(part, d, o_ref):
    for p in range(8):
        s = slice(p * 64, (p + 1) * 64)
        v = part[s, :] + d[s, :]
        o_ref[2 * p] = v[:, 0:64]
        o_ref[2 * p + 1] = v[:, 64:128]


def last(part, d):
    return pl.pallas_call(
        last_kernel,
        out_shape=jax.ShapeDtypeStruct((SHARE, BS, BS), F32),
        in_specs=[VM] * 2,
        out_specs=VM,
        compiler_params=params(),
        cost_estimate=cost(0, 2**21),
    )(part, d)


def to_group(x, axis, groups):
    return lax.all_to_all(x, axis, 0, 0, axis_index_groups=groups)


Z_GROUPS = [[z * 4 + c for z in range(3)] for c in range(4)]
X_GROUPS = [[z * 4 + c for c in range(4)] for z in range(3)]


def along_x(x, k):
    return lax.ppermute(x, "col", [(z * 4 + c, z * 4 + (c + k) % 4) for z in range(3) for c in range(4)])


def along_z(x, k):
    return lax.ppermute(x, "row", [(z * 2 + c, (z + k) % 4 * 2 + c) for z in range(4) for c in range(2)])


def along_depth(x, k):
    return lax.ppermute(x, "depth", [(i, (i + k) % LAYERS) for i in range(LAYERS)])


def per_device(left_blocks, right_blocks, triples):
    me, col, row = lax.axis_index("depth"), lax.axis_index("col"), lax.axis_index("row")
    where = jnp.stack([me, col, row]).astype(jnp.int32)
    l3, l = pack_left(left_blocks)
    zs = to_group(l3, "col", Z_GROUPS)
    r = pack_right(right_blocks)
    tab = table(triples)
    own_x = [along_x(l, k) for k in (1, 2, 3)]
    ls = split_own(where, l, *own_x)
    zs, ls, tab, r, where = lax.optimization_barrier((zs, ls, tab, r, where))
    xs = to_group(spread(where, zs), "col", X_GROUPS)
    rk = [r] + [along_z(r, k) for k in (1, 2, 3)]
    ls = split_others(where, ls, xs)
    rk, ls = lax.optimization_barrier((rk, ls))
    s4 = lax.ppermute(jnp.stack(rk), "row", [(i, i ^ 1) for i in range(8)])
    rs = last_right(where, first_right(where, rk), s4)
    p3 = shares(where, tab, ls, rs, (3, 1), where)
    m3 = shares(where, tab, ls, rs, (-3, -1), p3)
    f0, f1 = far(where, tab, ls, rs, m3)
    q1, q2 = along_depth(p3, 1), along_depth(m3, -1)
    q3, q4 = along_depth(f0, 2), along_depth(f1, -2)
    near = shares(where, tab, ls, rs, (2, -2, 0), f0)
    u = merge(up_kernel, near, q1, q3, weight=2**22)
    d = merge(down_kernel, near, q2, q4, u, weight=2**20)
    u, d = along_depth(u, 2), along_depth(d, -2)
    return last(partial_sum(near, q1, q2, u), d)


def solution(mesh):
    placed = (
        P(("row", "col", "depth"), None, None),
        P(("row", "col", "depth"), None, None),
        P(None, ("row", "col", "depth")),
    )
    return jax.shard_map(
        per_device,
        mesh=mesh,
        in_specs=placed,
        out_specs=P(("row", "col", "depth"), None, None),
        check_vma=False,
    )
```

time: 154 us -> 136 us (0.88)
  the two profiles are of different devices: /device:TPU:72 before, /device:TPU:82 now
where the time goes in v2:
time: 136 us; the launch traced here: 135 us
  starting transfers between devices  67.2 us (49%)
  waiting for transfers between devices  36.8 us (27%)
  Pallas kernels  21 us (15%)
  local copies, waits for them, and re-layouts  8.34 us (6%)
    ppermute x6, starting transfers between devices, along_depth(): lax.ppermute(x, 'depth', [(i, (i + k) % LAYERS) for i in range(LAYERS)])  23.2 us
    all_to_all x2, starting transfers between devices, to_group(): return lax.all_to_all(x, axis, 0, 0, axis_index_groups=groups)  18 us
    ppermute x6, waiting for transfers between devices, along_depth(): lax.ppermute(x, 'depth', [(i, (i + k) % LAYERS) for i in range(LAYERS)])  17.1 us
    ppermute x3, starting transfers between devices, along_z(): lax.ppermute(x, 'row', [(z * 2 + c, (z + k) % 4 * 2 + c) for z in range(4...  13.7 us
    ppermute x3, starting transfers between devices, along_x(): lax.ppermute(x, 'col', [(z * 4 + c, z * 4 + (c + k) % 4) for z in range(3...  10.5 us
    all_to_all x2, waiting for transfers between devices, to_group(): return lax.all_to_all(x, axis, 0, 0, axis_index_groups=groups)  9.89 us
    unnamed x24, local copies, waits for them, and re-layouts  8.34 us
    pallas_call x3, Pallas kernels, shares(): pl.pallas_call(kernel, out_shape=jax.ShapeDtypeStruct((512 * len(offsets)...  6.7 us
  transfers between devices with their start and end apart: 15, of which 10 were waited for; matrix products, arithmetic and copies ran while one was open for 0% of the time, Pallas kernels for 11%

profile of v2, /device:TPU:82, one launch (start us, length us, event | category | flops | bytes accessed | tf_op | source)
XLA Modules:
  0.0 134.8 jit_solution(4570560968463753368)
XLA Ops:
  0.0 1.1 copy-done.2
  1.1 1.1 shard_map.37
  2.2 13.0 %all-to-all-start = ((f32[3,256,256]{2,1,0:T(8,128)}), f32[3,256,256]{2,1,0:T(8,128)}, u32[]{:S(2)}, u32[]{:S(2)}) async-start(f32[3,256,256]{2,1,0:T(8,128)} %get-tuple-element.19), calls=%async_computation | async-start | bytes 1572864 | tf_op jit(solution)/shard_map/all_to_all | solution.py:331
  15.2 3.4 %collective-permute-start = (f32[256,256]{1,0:T(8,128)S(1)}, f32[256,256]{1,0:T(8,128)S(1)}, u32[]{:S(2)}, u32[]{:S(2)}) collective-permute-start(f32[256,256]{1,0:T(8,128)S(1)} %get-tuple-element.20.l0), channel_id=1, source_target_pairs={{0,8},{8,16},{16,24},{24,0},{32,40},{40,48},{48,56},{56,32},{64,72... | collective-permute-start | bytes 786440 | tf_op jit(solution)/shard_map/ppermute | solution.py:339
  18.6 3.0 %collective-permute-start.1 = (f32[256,256]{1,0:T(8,128)S(1)}, f32[256,256]{1,0:T(8,128)S(1)}, u32[]{:S(2)}, u32[]{:S(2)}) collective-permute-start(f32[256,256]{1,0:T(8,128)S(1)} %get-tuple-element.20.l0), channel_id=1, source_target_pairs={{0,16},{8,24},{16,0},{24,8},{32,48},{40,56},{48,32},{56,40},{64,80... | collective-permute-start | bytes 786440 | tf_op jit(solution)/shard_map/ppermute | solution.py:339
  21.6 4.1 %collective-permute-start.2 = (f32[256,256]{1,0:T(8,128)S(1)}, f32[256,256]{1,0:T(8,128)S(1)}, u32[]{:S(2)}, u32[]{:S(2)}) collective-permute-start(f32[256,256]{1,0:T(8,128)S(1)} %get-tuple-element.20.l0), channel_id=1, source_target_pairs={{0,24},{8,0},{16,8},{24,16},{32,56},{40,32},{48,40},{56,48},{64,88... | collective-permute-start | bytes 786440 | tf_op jit(solution)/shard_map/ppermute | solution.py:339
  25.7 0.1 shard_map.40.refs_0_
  25.9 4.9 %shard_map.39.tab = s32[136]{0:T(256)S(1)} custom-call(s32[3,512]{1,0:T(4,128)S(1)} %copy-done.11), custom_call_target="tpu_custom_call" | custom-call | bytes 8388608 | tf_op jit(solution)/shard_map/pallas_call | solution.py:86
  30.9 0.7 copy-done.5
  31.6 0.7 copy-done.7
  32.3 2.8 %collective-permute-done.2.lc = f32[256,256]{1,0:T(8,128)S(1)} collective-permute-done((f32[256,256]{1,0:T(8,128)S(1)}, f32[256,256]{1,0:T(8,128)S(1)}, u32[]{:S(2)}, u32[]{:S(2)}) %collective-permute-start.2) | collective-permute-done | bytes 262176 | tf_op jit(solution)/shard_map/ppermute | solution.py:339
  35.1 0.7 copy-done.9
  35.8 0.9 copy-done.4
  36.8 0.9 copy-done.6
  37.7 0.9 copy-done.8
  38.7 0.9 copy-done.10
  39.6 0.7 shard_map.38.ls_in
  40.3 0.2 all-to-all-done.zs
  40.5 1.3 shard_map.41
  41.8 1.3 copy-done
  43.1 5.0 %all-to-all-start.1 = ((f32[4,512,256]{2,1,0:T(8,128)}), f32[4,512,256]{2,1,0:T(8,128)}, u32[]{:S(2)}, u32[]{:S(2)}) async-start(f32[4,512,256]{2,1,0:T(8,128)} %copy-done), calls=%async_computation.1 | async-start | bytes 4194304 | tf_op jit(solution)/shard_map/all_to_all | solution.py:331
  48.0 5.3 %collective-permute-start.3 = (f32[256,256]{1,0:T(8,128)S(1)}, f32[256,256]{1,0:T(8,128)}, u32[]{:S(2)}, u32[]{:S(2)}) collective-permute-start(f32[256,256]{1,0:T(8,128)S(1)} %shard_map.40.refs_0_), channel_id=1, source_target_pairs={{0,192},{96,288},{192,384},{288,480},{384,576},{480,672},{576,0},{... | collective-permute-start | bytes 786440 | tf_op jit(solution)/shard_map/ppermute | solution.py:343
  53.3 4.5 %collective-permute-start.4 = (f32[256,256]{1,0:T(8,128)S(1)}, f32[256,256]{1,0:T(8,128)}, u32[]{:S(2)}, u32[]{:S(2)}) collective-permute-start(f32[256,256]{1,0:T(8,128)S(1)} %shard_map.40.refs_0_), channel_id=1, source_target_pairs={{0,384},{96,480},{192,576},{288,672},{384,0},{480,96},{576,192},{6... | collective-permute-start | bytes 786440 | tf_op jit(solution)/shard_map/ppermute | solution.py:343
  57.8 3.9 %collective-permute-start.5 = (f32[256,256]{1,0:T(8,128)S(1)}, f32[256,256]{1,0:T(8,128)}, u32[]{:S(2)}, u32[]{:S(2)}) collective-permute-start(f32[256,256]{1,0:T(8,128)S(1)} %shard_map.40.refs_0_), channel_id=1, source_target_pairs={{0,576},{96,672},{192,0},{288,96},{384,192},{480,288},{576,384},{6... | collective-permute-start | bytes 786440 | tf_op jit(solution)/shard_map/ppermute | solution.py:343
  61.7 9.7 %all-to-all-done.1.xs = f32[4,512,256]{2,1,0:T(8,128)} async-done(((f32[4,512,256]{2,1,0:T(8,128)}), f32[4,512,256]{2,1,0:T(8,128)}, u32[]{:S(2)}, u32[]{:S(2)}) %all-to-all-start.1) | async-done | bytes 2097184 | tf_op jit(solution)/shard_map/all_to_all | solution.py:331
  71.5 1.8 %shard_map.42.ls = bf16[48,128,256]{2,1,0:T(8,128)(2,1)S(1)} custom-call(s32[3]{0:T(128)S(1)} %pad_add_fusion.where.after_ref, bf16[48,128,256]{2,1,0:T(8,128)(2,1)S(1)} %shard_map.38.ls_in, f32[4,512,256]{2,1,0:T(8,128)} %all-to-all-done.1.xs), custom_call_target="tpu_custom_call", output_to_operand_aliasing={{}: (1, {})} | custom-call | bytes 4194304 | tf_op jit(solution)/shard_map/pallas_call | solution.py:192
  73.3 1.2 collective-permute-done.4.refs_2_
  74.5 4.5 %collective-permute-done.5.refs_3_ = f32[256,256]{1,0:T(8,128)} collective-permute-done((f32[256,256]{1,0:T(8,128)S(1)}, f32[256,256]{1,0:T(8,128)}, u32[]{:S(2)}, u32[]{:S(2)}) %collective-permute-start.5) | collective-permute-done | bytes 262176 | tf_op jit(solution)/shard_map/ppermute | solution.py:343
  79.1 1.2 pad_maximum_fusion
  80.3 1.9 %collective-permute-start.6 = (f32[4,256,256]{2,1,0:T(8,128)S(1)}, f32[4,256,256]{2,1,0:T(8,128)S(1)}, u32[]{:S(2)}, u32[]{:S(2)}) collective-permute-start(f32[4,256,256]{2,1,0:T(8,128)S(1)} %pad_maximum_fusion), channel_id=1, source_target_pairs={{0,96},{96,0},{192,288},{288,192},{384,480},{480,384},{576,672},{6... | collective-permute-start | bytes 3145736 | tf_op jit(solution)/shard_map/ppermute | solution.py:364
  82.2 1.4 %shard_map.43.rs_in = bf16[32,256,128]{2,1,0:T(8,128)(2,1)S(1)} custom-call(s32[3]{0:T(128)S(1)} %pad_add_fusion.where.after_ref, f32[256,256]{1,0:T(8,128)S(1)} %shard_map.40.refs_0_, f32[256,256]{1,0:T(8,128)} %collective-permute-done.3.refs_1_, f32[256,256]{1,0:T(8,128)} %collective-permute-done.4.refs_2_, f32[256,256]{1,0:T(8,128)} %collective-permute-done.5.refs_3_), custom_call_target="tpu_custom_call" | custom-call | bytes 4194304 | tf_op jit(solution)/shard_map/pallas_call | solution.py:211
  83.6 1.2 collective-permute-done.6.s4
  84.8 0.8 shard_map.44.rs
  85.6 2.0 %shard_map.45.after_ref = f32[1024,128]{1,0:T(8,128)S(1)} custom-call(s32[3]{0:T(128)S(1)} %pad_add_fusion.where.after_ref, s32[136]{0:T(256)S(1)} %shard_map.39.tab, bf16[48,128,256]{2,1,0:T(8,128)(2,1)S(1)} %shard_map.42.ls, bf16[32,256,128]{2,1,0:T(8,128)(2,1)S(1)} %shard_map.44.rs, s32[3]{0:T(128)S(1)} %pad_add_fusion.where.after_ref), custom_call_target="tpu_custom_call" | custom-call | flops 268435456 | bytes 2097152 | tf_op jit(solution)/shard_map/pallas_call | solution.py:248
  87.6 3.5 %collective-permute-start.7 = (f32[1024,128]{1,0:T(8,128)S(1)}, f32[1024,128]{1,0:T(8,128)S(1)}, u32[]{:S(2)}, u32[]{:S(2)}) collective-permute-start(f32[1024,128]{1,0:T(8,128)S(1)} %shard_map.45.after_ref), channel_id=1, source_target_pairs={{0,1},{1,2},{2,3},{3,4},{4,5},{5,6},{6,7},{7,0},{8,9},{9,10},{10,1... | collective-permute-start | bytes 1572872 | tf_op jit(solution)/shard_map/ppermute | solution.py:347
  91.1 2.0 %shard_map.46.after_ref = f32[1024,128]{1,0:T(8,128)S(1)} custom-call(s32[3]{0:T(128)S(1)} %pad_add_fusion.where.after_ref, s32[136]{0:T(256)S(1)} %shard_map.39.tab, bf16[48,128,256]{2,1,0:T(8,128)(2,1)S(1)} %shard_map.42.ls, bf16[32,256,128]{2,1,0:T(8,128)(2,1)S(1)} %shard_map.44.rs, f32[1024,128]{1,0:T(8,128)S(1)} %shard_map.45.after_ref), custom_call_target="tpu_custom_call" | custom-call | flops 268435456 | bytes 2097152 | tf_op jit(solution)/shard_map/pallas_call | solution.py:248
  93.1 2.4 %collective-permute-start.8 = (f32[1024,128]{1,0:T(8,128)S(1)}, f32[1024,128]{1,0:T(8,128)S(1)}, u32[]{:S(2)}, u32[]{:S(2)}) collective-permute-start(f32[1024,128]{1,0:T(8,128)S(1)} %shard_map.46.after_ref), channel_id=1, source_target_pairs={{0,7},{1,0},{2,1},{3,2},{4,3},{5,4},{6,5},{7,6},{8,15},{9,8},{10,9... | collective-permute-start | bytes 1572872 | tf_op jit(solution)/shard_map/ppermute | solution.py:347
  95.5 1.1 shard_map.47
  96.5 6.9 %collective-permute-start.9 = (f32[256,128]{1,0:T(8,128)S(1)}, f32[256,128]{1,0:T(8,128)S(1)}, u32[]{:S(2)}, u32[]{:S(2)}) collective-permute-start(f32[256,128]{1,0:T(8,128)S(1)} %get-tuple-element.31.after_ref), channel_id=1, source_target_pairs={{0,2},{1,3},{2,4},{3,5},{4,6},{5,7},{6,0},{7,1},{8,10},{9,11},{10,... | collective-permute-start | bytes 393224 | tf_op jit(solution)/shard_map/ppermute | solution.py:347
  103.4 1.9 %collective-permute-start.11 = (f32[256,128]{1,0:T(8,128)S(1)}, f32[256,128]{1,0:T(8,128)S(1)}, u32[]{:S(2)}, u32[]{:S(2)}) collective-permute-start(f32[256,128]{1,0:T(8,128)S(1)} %get-tuple-element.32), channel_id=1, source_target_pairs={{0,6},{1,7},{2,0},{3,1},{4,2},{5,3},{6,4},{7,5},{8,14},{9,15},{10,... | collective-permute-start | bytes 393224 | tf_op jit(solution)/shard_map/ppermute | solution.py:347
  105.4 2.7 %shard_map.48.near = f32[1536,128]{1,0:T(8,128)S(1)} custom-call(s32[3]{0:T(128)S(1)} %pad_add_fusion.where.after_ref, s32[136]{0:T(256)S(1)} %shard_map.39.tab, bf16[48,128,256]{2,1,0:T(8,128)(2,1)S(1)} %shard_map.42.ls, bf16[32,256,128]{2,1,0:T(8,128)(2,1)S(1)} %shard_map.44.rs, f32[256,128]{1,0:T(8,128)S(1)} %get-tuple-element.31.after_ref), custom_call_target="tpu_custom_call" | custom-call | flops 402653184 | bytes 3145728 | tf_op jit(solution)/shard_map/pallas_call | solution.py:248
  108.1 0.3 collective-permute-done.9.half
  108.5 6.6 %collective-permute-start.10 = (f32[512,128]{1,0:T(8,128)S(1)}, f32[512,128]{1,0:T(8,128)S(1)}, u32[]{:S(2)}, u32[]{:S(2)}) collective-permute-start(f32[512,128]{1,0:T(8,128)S(1)} %shard_map.49.after_ref), channel_id=1, source_target_pairs={{0,2},{1,3},{2,4},{3,5},{4,6},{5,7},{6,0},{7,1},{8,10},{9,11},{10,... | collective-permute-start | bytes 786440 | tf_op jit(solution)/shard_map/ppermute | solution.py:347
  115.1 2.7 %collective-permute-done.11.half = f32[256,128]{1,0:T(8,128)S(1)} collective-permute-done((f32[256,128]{1,0:T(8,128)S(1)}, f32[256,128]{1,0:T(8,128)S(1)}, u32[]{:S(2)}, u32[]{:S(2)}) %collective-permute-start.11) | collective-permute-done | bytes 131104 | tf_op jit(solution)/shard_map/ppermute | solution.py:347
  117.8 1.9 %collective-permute-start.12 = (f32[512,128]{1,0:T(8,128)S(1)}, f32[512,128]{1,0:T(8,128)S(1)}, u32[]{:S(2)}, u32[]{:S(2)}) collective-permute-start(f32[512,128]{1,0:T(8,128)S(1)} %shard_map.51), channel_id=1, source_target_pairs={{0,6},{1,7},{2,0},{3,1},{4,2},{5,3},{6,4},{7,5},{8,14},{9,15},{10,... | collective-permute-start | bytes 786440 | tf_op jit(solution)/shard_map/ppermute | solution.py:347
  119.7 4.8 %collective-permute-done.10.u = f32[512,128]{1,0:T(8,128)S(1)} collective-permute-done((f32[512,128]{1,0:T(8,128)S(1)}, f32[512,128]{1,0:T(8,128)S(1)}, u32[]{:S(2)}, u32[]{:S(2)}) %collective-permute-start.10) | collective-permute-done | bytes 262176 | tf_op jit(solution)/shard_map/ppermute | solution.py:347
  124.6 9.3 %collective-permute-done.12.d = f32[512,128]{1,0:T(8,128)S(1)} collective-permute-done((f32[512,128]{1,0:T(8,128)S(1)}, f32[512,128]{1,0:T(8,128)S(1)}, u32[]{:S(2)}, u32[]{:S(2)}) %collective-permute-start.12) | collective-permute-done | bytes 262176 | tf_op jit(solution)/shard_map/ppermute | solution.py:347
  133.9 0.9 shard_map.52
  (24 shorter events, 0.3 us)
Async XLA Ops:
  0.0 25.7 %copy-start.1 = (f32[16,64,64]{2,1,0:T(8,128)S(1)}, f32[16,64,64]{2,1,0:T(8,128)}, u32[]{:S(2)}) copy-start(f32[16,64,64]{2,1,0:T(8,128)} %r_ref.1) | copy-start | bytes 786436
  0.0 1.1 copy-start.2
  1.1 24.8 %copy-start.11 = (s32[3,512]{1,0:T(4,128)S(1)}, s32[3,512]{1,0:T(4,128)}, u32[]{:S(2)}) copy-start(s32[3,512]{1,0:T(4,128)} %t_ref.1) | copy-start | bytes 18436
  2.2 29.4 %copy-start.3 = (f32[256,256]{1,0:T(8,128)}, f32[256,256]{1,0:T(8,128)S(1)}, u32[]{:S(2)}) copy-start(f32[256,256]{1,0:T(8,128)S(1)} %get-tuple-element.20.l0) | copy-start | bytes 786436
  2.2 38.3 %all-to-all-start = ((f32[3,256,256]{2,1,0:T(8,128)}), f32[3,256,256]{2,1,0:T(8,128)}, u32[]{:S(2)}, u32[]{:S(2)}) async-start(f32[3,256,256]{2,1,0:T(8,128)} %get-tuple-element.19), calls=%async_computation | async-start | bytes 1572864 | tf_op jit(solution)/shard_map/all_to_all | solution.py:331
  15.2 15.7 %collective-permute-start = (f32[256,256]{1,0:T(8,128)S(1)}, f32[256,256]{1,0:T(8,128)S(1)}, u32[]{:S(2)}, u32[]{:S(2)}) collective-permute-start(f32[256,256]{1,0:T(8,128)S(1)} %get-tuple-element.20.l0), channel_id=1, source_target_pairs={{0,8},{8,16},{16,24},{24,0},{32,40},{40,48},{48,56},{56,32},{64,72... | collective-permute-start | bytes 786440 | tf_op jit(solution)/shard_map/ppermute | solution.py:339
  18.6 13.0 %collective-permute-start.1 = (f32[256,256]{1,0:T(8,128)S(1)}, f32[256,256]{1,0:T(8,128)S(1)}, u32[]{:S(2)}, u32[]{:S(2)}) collective-permute-start(f32[256,256]{1,0:T(8,128)S(1)} %get-tuple-element.20.l0), channel_id=1, source_target_pairs={{0,16},{8,24},{16,0},{24,8},{32,48},{40,56},{48,32},{56,40},{64,80... | collective-permute-start | bytes 786440 | tf_op jit(solution)/shard_map/ppermute | solution.py:339
  21.6 13.5 %collective-permute-start.2 = (f32[256,256]{1,0:T(8,128)S(1)}, f32[256,256]{1,0:T(8,128)S(1)}, u32[]{:S(2)}, u32[]{:S(2)}) collective-permute-start(f32[256,256]{1,0:T(8,128)S(1)} %get-tuple-element.20.l0), channel_id=1, source_target_pairs={{0,24},{8,0},{16,8},{24,16},{32,56},{40,32},{48,40},{56,48},{64,88... | collective-permute-start | bytes 786440 | tf_op jit(solution)/shard_map/ppermute | solution.py:339
  30.9 0.7 copy-start.5
  31.6 0.7 copy-start.7
  35.1 0.7 copy-start.9
  35.8 0.9 copy-start.4
  36.8 0.9 copy-start.6
  37.7 0.9 copy-start.8
  38.7 0.9 copy-start.10
  41.8 1.3 copy-start
  43.1 28.4 %all-to-all-start.1 = ((f32[4,512,256]{2,1,0:T(8,128)}), f32[4,512,256]{2,1,0:T(8,128)}, u32[]{:S(2)}, u32[]{:S(2)}) async-start(f32[4,512,256]{2,1,0:T(8,128)} %copy-done), calls=%async_computation.1 | async-start | bytes 4194304 | tf_op jit(solution)/shard_map/all_to_all | solution.py:331
  48.0 25.3 %collective-permute-start.3 = (f32[256,256]{1,0:T(8,128)S(1)}, f32[256,256]{1,0:T(8,128)}, u32[]{:S(2)}, u32[]{:S(2)}) collective-permute-start(f32[256,256]{1,0:T(8,128)S(1)} %shard_map.40.refs_0_), channel_id=1, source_target_pairs={{0,192},{96,288},{192,384},{288,480},{384,576},{480,672},{576,0},{... | collective-permute-start | bytes 786440 | tf_op jit(solution)/shard_map/ppermute | solution.py:343
  53.3 21.2 %collective-permute-start.4 = (f32[256,256]{1,0:T(8,128)S(1)}, f32[256,256]{1,0:T(8,128)}, u32[]{:S(2)}, u32[]{:S(2)}) collective-permute-start(f32[256,256]{1,0:T(8,128)S(1)} %shard_map.40.refs_0_), channel_id=1, source_target_pairs={{0,384},{96,480},{192,576},{288,672},{384,0},{480,96},{576,192},{6... | collective-permute-start | bytes 786440 | tf_op jit(solution)/shard_map/ppermute | solution.py:343
  57.8 21.3 %collective-permute-start.5 = (f32[256,256]{1,0:T(8,128)S(1)}, f32[256,256]{1,0:T(8,128)}, u32[]{:S(2)}, u32[]{:S(2)}) collective-permute-start(f32[256,256]{1,0:T(8,128)S(1)} %shard_map.40.refs_0_), channel_id=1, source_target_pairs={{0,576},{96,672},{192,0},{288,96},{384,192},{480,288},{576,384},{6... | collective-permute-start | bytes 786440 | tf_op jit(solution)/shard_map/ppermute | solution.py:343
  80.3 4.6 %collective-permute-start.6 = (f32[4,256,256]{2,1,0:T(8,128)S(1)}, f32[4,256,256]{2,1,0:T(8,128)S(1)}, u32[]{:S(2)}, u32[]{:S(2)}) collective-permute-start(f32[4,256,256]{2,1,0:T(8,128)S(1)} %pad_maximum_fusion), channel_id=1, source_target_pairs={{0,96},{96,0},{192,288},{288,192},{384,480},{480,384},{576,672},{6... | collective-permute-start | bytes 3145736 | tf_op jit(solution)/shard_map/ppermute | solution.py:364
  87.6 20.8 %collective-permute-start.7 = (f32[1024,128]{1,0:T(8,128)S(1)}, f32[1024,128]{1,0:T(8,128)S(1)}, u32[]{:S(2)}, u32[]{:S(2)}) collective-permute-start(f32[1024,128]{1,0:T(8,128)S(1)} %shard_map.45.after_ref), channel_id=1, source_target_pairs={{0,1},{1,2},{2,3},{3,4},{4,5},{5,6},{6,7},{7,0},{8,9},{9,10},{10,1... | collective-permute-start | bytes 1572872 | tf_op jit(solution)/shard_map/ppermute | solution.py:347
  93.1 24.6 %collective-permute-start.8 = (f32[1024,128]{1,0:T(8,128)S(1)}, f32[1024,128]{1,0:T(8,128)S(1)}, u32[]{:S(2)}, u32[]{:S(2)}) collective-permute-start(f32[1024,128]{1,0:T(8,128)S(1)} %shard_map.46.after_ref), channel_id=1, source_target_pairs={{0,7},{1,0},{2,1},{3,2},{4,3},{5,4},{6,5},{7,6},{8,15},{9,8},{10,9... | collective-permute-start | bytes 1572872 | tf_op jit(solution)/shard_map/ppermute | solution.py:347
  96.5 11.9 %collective-permute-start.9 = (f32[256,128]{1,0:T(8,128)S(1)}, f32[256,128]{1,0:T(8,128)S(1)}, u32[]{:S(2)}, u32[]{:S(2)}) collective-permute-start(f32[256,128]{1,0:T(8,128)S(1)} %get-tuple-element.31.after_ref), channel_id=1, source_target_pairs={{0,2},{1,3},{2,4},{3,5},{4,6},{5,7},{6,0},{7,1},{8,10},{9,11},{10,... | collective-permute-start | bytes 393224 | tf_op jit(solution)/shard_map/ppermute | solution.py:347
  103.4 14.3 %collective-permute-start.11 = (f32[256,128]{1,0:T(8,128)S(1)}, f32[256,128]{1,0:T(8,128)S(1)}, u32[]{:S(2)}, u32[]{:S(2)}) collective-permute-start(f32[256,128]{1,0:T(8,128)S(1)} %get-tuple-element.32), channel_id=1, source_target_pairs={{0,6},{1,7},{2,0},{3,1},{4,2},{5,3},{6,4},{7,5},{8,14},{9,15},{10,... | collective-permute-start | bytes 393224 | tf_op jit(solution)/shard_map/ppermute | solution.py:347
  108.5 16.1 %collective-permute-start.10 = (f32[512,128]{1,0:T(8,128)S(1)}, f32[512,128]{1,0:T(8,128)S(1)}, u32[]{:S(2)}, u32[]{:S(2)}) collective-permute-start(f32[512,128]{1,0:T(8,128)S(1)} %shard_map.49.after_ref), channel_id=1, source_target_pairs={{0,2},{1,3},{2,4},{3,5},{4,6},{5,7},{6,0},{7,1},{8,10},{9,11},{10,... | collective-permute-start | bytes 786440 | tf_op jit(solution)/shard_map/ppermute | solution.py:347
  117.8 16.1 %collective-permute-start.12 = (f32[512,128]{1,0:T(8,128)S(1)}, f32[512,128]{1,0:T(8,128)S(1)}, u32[]{:S(2)}, u32[]{:S(2)}) collective-permute-start(f32[512,128]{1,0:T(8,128)S(1)} %shard_map.51), channel_id=1, source_target_pairs={{0,6},{1,7},{2,0},{3,1},{4,2},{5,3},{6,4},{7,5},{8,14},{9,15},{10,... | collective-permute-start | bytes 786440 | tf_op jit(solution)/shard_map/ppermute | solution.py:347

commit v3 on v2

--- a/solution.py
+++ b/solution.py
@@ -130,34 +130,28 @@
 
 
 def share_into(tab, first, o_ref, at, count, ls, rs):
-    def step(p, c):
-        for q in range(4):
-            n = p * 4 + q
-            o_ref[pl.ds(at + n * 64, 64), :] = two_slots(first + 2 * n, tab, ls, rs)
-        return c
-
-    lax.fori_loop(0, count // 4, step, 0)
+    for n in range(count):
+        o_ref[at + n * 64 : at + (n + 1) * 64, :] = two_slots(first + 2 * n, tab, ls, rs)
 
 
 LEFT = jax.ShapeDtypeStruct((48, 128, 256), BF16)
 RIGHT = jax.ShapeDtypeStruct((32, 256, 128), BF16)
 
 
-def split_own_kernel(where, l0, la, lb, lc, ls):
-    z, x = where[1] >> 2, where[1] & 3
-    for k, ref in enumerate((l0, la, lb, lc)):
-        prep_left(ref, ls, z * 4 + ((x + 4 - k) & 3))
-
-
-def split_own(where, *parts):
-    return pl.pallas_call(
-        split_own_kernel,
+def split_one(where, k, part, *so_far):
+    def kernel(where, part, *rest):
+        z, x = where[1] >> 2, where[1] & 3
+        prep_left(part, rest[-1], z * 4 + ((x + 4 - k) & 3))
+
+    return pl.pallas_call(
+        kernel,
         out_shape=LEFT,
-        in_specs=[SM] + [VM] * 4,
-        out_specs=VM,
-        compiler_params=params(),
-        cost_estimate=cost(0, 2**22),
-    )(where, *parts)
+        in_specs=[SM] + [VM] * (1 + len(so_far)),
+        out_specs=VM,
+        input_output_aliases={2: 0} if so_far else {},
+        compiler_params=params(),
+        cost_estimate=cost(0, 2**20),
+    )(where, part, *so_far)
 
 
 def spread_kernel(where, zs, o_ref):
@@ -200,32 +194,32 @@
     )(where, ls, xs)
 
 
-def first_right_kernel(where, *refs):
-    r4, rs = refs[:4], refs[4]
-    core = where[2] & 1
-    for k in range(4):
-        prep_right(r4[k], rs, (((where[2] >> 1) + 4 - k) & 3) * 2 + core)
-
-
-def first_right(where, r4):
+def first_right_kernel(where, r, sibling, r1, r2, r3, rs):
+    z, core = where[2] >> 1, where[2] & 1
+    prep_right(sibling, rs, z * 2 + 1 - core)
+    for k, ref in enumerate((r, r1, r2, r3)):
+        prep_right(ref, rs, ((z + 4 - k) & 3) * 2 + core)
+
+
+def first_right(where, *parts):
     return pl.pallas_call(
         first_right_kernel,
         out_shape=RIGHT,
-        in_specs=[SM] + [VM] * 4,
+        in_specs=[SM] + [VM] * 5,
         out_specs=VM,
         compiler_params=params(),
         cost_estimate=cost(0, 2**22),
-    )(where, *r4)
+    )(where, *parts)
 
 
 def share_of(where, k):
     return ((where[0] + 8 + k) & 7) * SHARE
 
 
-def last_right_kernel(where, rs_in, s4, rs):
-    core = where[2] & 1
-    for k in range(4):
-        prep_right(s4.at[k], rs, (((where[2] >> 1) + 4 - k) & 3) * 2 + 1 - core)
+def last_right_kernel(where, rs_in, s3, rs):
+    z, core = where[2] >> 1, where[2] & 1
+    for k in range(3):
+        prep_right(s3.at[k], rs, ((z + 3 - k) & 3) * 2 + 1 - core)
 
 
 def last_right(where, rs, s4):
@@ -341,6 +335,10 @@
 
 def along_z(x, k):
     return lax.ppermute(x, "row", [(z * 2 + c, (z + k) % 4 * 2 + c) for z in range(4) for c in range(2)])
+
+
+def swap_core(x):
+    return lax.ppermute(x, "row", [(i, i ^ 1) for i in range(8)])
 
 
 def along_depth(x, k):
@@ -354,15 +352,17 @@
     zs = to_group(l3, "col", Z_GROUPS)
     r = pack_right(right_blocks)
     tab = table(triples)
-    own_x = [along_x(l, k) for k in (1, 2, 3)]
-    ls = split_own(where, l, *own_x)
-    zs, ls, tab, r, where = lax.optimization_barrier((zs, ls, tab, r, where))
+    sibling = swap_core(r)
+    ls = split_one(where, 0, l)
+    for k in (1, 2, 3):
+        ls = split_one(where, k, along_x(l, k), ls)
+    zs, ls, sibling, tab, r, where = lax.optimization_barrier((zs, ls, sibling, tab, r, where))
     xs = to_group(spread(where, zs), "col", X_GROUPS)
-    rk = [r] + [along_z(r, k) for k in (1, 2, 3)]
+    rk = [along_z(r, k) for k in (1, 2, 3)]
     ls = split_others(where, ls, xs)
     rk, ls = lax.optimization_barrier((rk, ls))
-    s4 = lax.ppermute(jnp.stack(rk), "row", [(i, i ^ 1) for i in range(8)])
-    rs = last_right(where, first_right(where, rk), s4)
+    s3 = swap_core(jnp.stack(rk))
+    rs = last_right(where, first_right(where, r, sibling, *rk), s3)
     p3 = shares(where, tab, ls, rs, (3, 1), where)
     m3 = shares(where, tab, ls, rs, (-3, -1), p3)
     f0, f1 = far(where, tab, ls, rs, m3)

time: 136 us -> 135 us (level)
  the two profiles are of different devices: /device:TPU:82 before, /device:TPU:83 now
where the time goes in v3:
time: 135 us; the launch traced here: 134 us
  starting transfers between devices  69.1 us (51%)
  waiting for transfers between devices  37.9 us (28%)
  Pallas kernels  21.9 us (16%)
  local copies, waits for them, and re-layouts  3.37 us (2%)
    ppermute x6, starting transfers between devices, along_depth(): lax.ppermute(x, 'depth', [(i, (i + k) % LAYERS) for i in range(LAYERS)])  21.1 us
    ppermute x6, waiting for transfers between devices, along_depth(): lax.ppermute(x, 'depth', [(i, (i + k) % LAYERS) for i in range(LAYERS)])  20.9 us
    all_to_all x2, starting transfers between devices, to_group(): return lax.all_to_all(x, axis, 0, 0, axis_index_groups=groups)  18.3 us
    ppermute x3, starting transfers between devices, along_z(): lax.ppermute(x, 'row', [(z * 2 + c, (z + k) % 4 * 2 + c) for z in range(4...  14 us
    all_to_all x2, waiting for transfers between devices, to_group(): return lax.all_to_all(x, axis, 0, 0, axis_index_groups=groups)  9.64 us
    ppermute x3, starting transfers between devices, along_x(): lax.ppermute(x, 'col', [(z * 4 + c, z * 4 + (c + k) % 4) for z in range(3...  9.63 us
    ppermute x3, waiting for transfers between devices, along_z(): lax.ppermute(x, 'row', [(z * 2 + c, (z + k) % 4 * 2 + c) for z in range(4...  6.97 us
    ppermute x2, starting transfers between devices, swap_core(): return lax.ppermute(x, 'row', [(i, i ^ 1) for i in range(8)])  6.11 us
  transfers between devices with their start and end apart: 16, of which 7 were waited for; matrix products, arithmetic and copies ran while one was open for 0% of the time, Pallas kernels for 12%

profile of v3, /device:TPU:83, one launch (start us, length us, event | category | flops | bytes accessed | tf_op | source)
XLA Modules:
  0.0 133.8 jit_solution(13759812446132643817)
XLA Ops:
  0.0 1.0 copy-done.2
  1.0 1.1 shard_map.37
  2.2 12.7 %all-to-all-start = ((f32[3,256,256]{2,1,0:T(8,128)}), f32[3,256,256]{2,1,0:T(8,128)}, u32[]{:S(2)}, u32[]{:S(2)}) async-start(f32[3,256,256]{2,1,0:T(8,128)} %get-tuple-element.19), calls=%async_computation | async-start | bytes 1572864 | tf_op jit(solution)/shard_map/all_to_all | solution.py:325
  14.9 3.1 %collective-permute-start.2 = (f32[256,256]{1,0:T(8,128)}, f32[256,256]{1,0:T(8,128)}, u32[]{:S(2)}, u32[]{:S(2)}) collective-permute-start(f32[256,256]{1,0:T(8,128)} %get-tuple-element.20.part), channel_id=1, source_target_pairs={{0,8},{8,16},{16,24},{24,0},{32,40},{40,48},{48,56},{56,32},{64,72... | collective-permute-start | bytes 786440 | tf_op jit(solution)/shard_map/ppermute | solution.py:333
  18.0 2.7 %collective-permute-start.1 = (f32[256,256]{1,0:T(8,128)}, f32[256,256]{1,0:T(8,128)}, u32[]{:S(2)}, u32[]{:S(2)}) collective-permute-start(f32[256,256]{1,0:T(8,128)} %get-tuple-element.20.part), channel_id=1, source_target_pairs={{0,16},{8,24},{16,0},{24,8},{32,48},{40,56},{48,32},{56,40},{64,80... | collective-permute-start | bytes 786440 | tf_op jit(solution)/shard_map/ppermute | solution.py:333
  20.8 3.8 %collective-permute-start = (f32[256,256]{1,0:T(8,128)}, f32[256,256]{1,0:T(8,128)}, u32[]{:S(2)}, u32[]{:S(2)}) collective-permute-start(f32[256,256]{1,0:T(8,128)} %get-tuple-element.20.part), channel_id=1, source_target_pairs={{0,24},{8,0},{16,8},{24,16},{32,56},{40,32},{48,40},{56,48},{64,88... | collective-permute-start | bytes 786440 | tf_op jit(solution)/shard_map/ppermute | solution.py:333
  24.5 0.0 copy-start.1
  24.6 1.0 copy-done.1
  25.6 0.1 shard_map.42.r
  25.7 3.7 %collective-permute-start.3 = (f32[256,256]{1,0:T(8,128)S(1)}, f32[256,256]{1,0:T(8,128)}, u32[]{:S(2)}, u32[]{:S(2)}) collective-permute-start(f32[256,256]{1,0:T(8,128)S(1)} %shard_map.42.r), channel_id=1, source_target_pairs={{0,96},{96,0},{192,288},{288,192},{384,480},{480,384},{576,672},{6... | collective-permute-start | bytes 786440 | tf_op jit(solution)/shard_map/ppermute | solution.py:341
  29.5 0.1 pad_add_fusion.where.after_ref
  29.5 1.0 shard_map.38.rest_0_
  30.5 4.9 %shard_map.43.tab = s32[136]{0:T(256)S(1)} custom-call(s32[3,512]{1,0:T(4,128)S(1)} %copy-done.3), custom_call_target="tpu_custom_call" | custom-call | bytes 8388608 | tf_op jit(solution)/shard_map/pallas_call | solution.py:86
  35.5 0.0 collective-permute-done.2.part
  35.5 1.0 shard_map.39.rest_0_
  36.5 1.0 shard_map.40.rest_0_
  37.5 1.0 shard_map.41.ls_in
  38.5 1.3 shard_map.44
  39.9 1.3 copy-done
  41.1 5.6 %all-to-all-start.1 = ((f32[4,512,256]{2,1,0:T(8,128)}), f32[4,512,256]{2,1,0:T(8,128)}, u32[]{:S(2)}, u32[]{:S(2)}) async-start(f32[4,512,256]{2,1,0:T(8,128)} %copy-done), calls=%async_computation.1 | async-start | bytes 4194304 | tf_op jit(solution)/shard_map/all_to_all | solution.py:325
  46.7 4.4 %collective-permute-start.4 = (f32[256,256]{1,0:T(8,128)S(1)}, f32[256,256]{1,0:T(8,128)}, u32[]{:S(2)}, u32[]{:S(2)}) collective-permute-start(f32[256,256]{1,0:T(8,128)S(1)} %shard_map.42.r), channel_id=1, source_target_pairs={{0,192},{96,288},{192,384},{288,480},{384,576},{480,672},{576,0},{... | collective-permute-start | bytes 786440 | tf_op jit(solution)/shard_map/ppermute | solution.py:337
  51.2 6.2 %collective-permute-start.5 = (f32[256,256]{1,0:T(8,128)S(1)}, f32[256,256]{1,0:T(8,128)}, u32[]{:S(2)}, u32[]{:S(2)}) collective-permute-start(f32[256,256]{1,0:T(8,128)S(1)} %shard_map.42.r), channel_id=1, source_target_pairs={{0,384},{96,480},{192,576},{288,672},{384,0},{480,96},{576,192},{6... | collective-permute-start | bytes 786440 | tf_op jit(solution)/shard_map/ppermute | solution.py:337
  57.4 3.4 %collective-permute-start.6 = (f32[256,256]{1,0:T(8,128)S(1)}, f32[256,256]{1,0:T(8,128)}, u32[]{:S(2)}, u32[]{:S(2)}) collective-permute-start(f32[256,256]{1,0:T(8,128)S(1)} %shard_map.42.r), channel_id=1, source_target_pairs={{0,576},{96,672},{192,0},{288,96},{384,192},{480,288},{576,384},{6... | collective-permute-start | bytes 786440 | tf_op jit(solution)/shard_map/ppermute | solution.py:337
  60.7 9.6 %all-to-all-done.1.xs = f32[4,512,256]{2,1,0:T(8,128)} async-done(((f32[4,512,256]{2,1,0:T(8,128)}), f32[4,512,256]{2,1,0:T(8,128)}, u32[]{:S(2)}, u32[]{:S(2)}) %all-to-all-start.1) | async-done | bytes 2097184 | tf_op jit(solution)/shard_map/all_to_all | solution.py:325
  70.4 1.8 %shard_map.45.ls = bf16[48,128,256]{2,1,0:T(8,128)(2,1)S(1)} custom-call(s32[3]{0:T(128)S(1)} %pad_add_fusion.where.after_ref, bf16[48,128,256]{2,1,0:T(8,128)(2,1)S(1)} %shard_map.41.ls_in, f32[4,512,256]{2,1,0:T(8,128)} %all-to-all-done.1.xs), custom_call_target="tpu_custom_call", output_to_operand_aliasing={{}: (1, {})} | custom-call | bytes 4194304 | tf_op jit(solution)/shard_map/pallas_call | solution.py:186
  72.2 1.3 collective-permute-done.5.r2
  73.5 5.7 %collective-permute-done.6.r3 = f32[256,256]{1,0:T(8,128)} collective-permute-done((f32[256,256]{1,0:T(8,128)S(1)}, f32[256,256]{1,0:T(8,128)}, u32[]{:S(2)}, u32[]{:S(2)}) %collective-permute-start.6) | collective-permute-done | bytes 262176 | tf_op jit(solution)/shard_map/ppermute | solution.py:337
  79.2 1.2 pad_maximum_fusion
  80.3 2.4 %collective-permute-start.7 = (f32[3,256,256]{2,1,0:T(8,128)S(1)}, f32[3,256,256]{2,1,0:T(8,128)S(1)}, u32[]{:S(2)}, u32[]{:S(2)}) collective-permute-start(f32[3,256,256]{2,1,0:T(8,128)S(1)} %pad_maximum_fusion), channel_id=1, source_target_pairs={{0,96},{96,0},{192,288},{288,192},{384,480},{480,384},{576,672},{6... | collective-permute-start | bytes 2359304 | tf_op jit(solution)/shard_map/ppermute | solution.py:341
  82.8 1.5 %shard_map.46.rs_in = bf16[32,256,128]{2,1,0:T(8,128)(2,1)S(1)} custom-call(s32[3]{0:T(128)S(1)} %pad_add_fusion.where.after_ref, f32[256,256]{1,0:T(8,128)S(1)} %shard_map.42.r, f32[256,256]{1,0:T(8,128)} %collective-permute-done.3.sibling, f32[256,256]{1,0:T(8,128)} %collective-permute-done.4.r1, f32[256,256]{1,0:T(8,128)} %collective-permute-done.5.r2, ...), custom_call_target="tpu_custom_call" | custom-call | bytes 4194304 | tf_op jit(solution)/shard_map/pallas_call | solution.py:205
  84.3 0.4 collective-permute-done.7.s3
  84.6 0.7 shard_map.47.rs
  85.4 1.3 shard_map.48.after_ref
  86.7 3.2 %collective-permute-start.8 = (f32[1024,128]{1,0:T(8,128)S(1)}, f32[1024,128]{1,0:T(8,128)S(1)}, u32[]{:S(2)}, u32[]{:S(2)}) collective-permute-start(f32[1024,128]{1,0:T(8,128)S(1)} %shard_map.48.after_ref), channel_id=1, source_target_pairs={{0,1},{1,2},{2,3},{3,4},{4,5},{5,6},{6,7},{7,0},{8,9},{9,10},{10,1... | collective-permute-start | bytes 1572872 | tf_op jit(solution)/shard_map/ppermute | solution.py:345
  89.9 1.3 shard_map.49.after_ref
  91.3 2.1 %collective-permute-start.9 = (f32[1024,128]{1,0:T(8,128)S(1)}, f32[1024,128]{1,0:T(8,128)S(1)}, u32[]{:S(2)}, u32[]{:S(2)}) collective-permute-start(f32[1024,128]{1,0:T(8,128)S(1)} %shard_map.49.after_ref), channel_id=1, source_target_pairs={{0,7},{1,0},{2,1},{3,2},{4,3},{5,4},{6,5},{7,6},{8,15},{9,8},{10,9... | collective-permute-start | bytes 1572872 | tf_op jit(solution)/shard_map/ppermute | solution.py:345
  93.3 1.1 shard_map.50
  94.4 6.6 %collective-permute-start.10 = (f32[256,128]{1,0:T(8,128)S(1)}, f32[256,128]{1,0:T(8,128)S(1)}, u32[]{:S(2)}, u32[]{:S(2)}) collective-permute-start(f32[256,128]{1,0:T(8,128)S(1)} %get-tuple-element.31.after_ref), channel_id=1, source_target_pairs={{0,2},{1,3},{2,4},{3,5},{4,6},{5,7},{6,0},{7,1},{8,10},{9,11},{10,... | collective-permute-start | bytes 393224 | tf_op jit(solution)/shard_map/ppermute | solution.py:345
  101.0 1.9 %collective-permute-start.12 = (f32[256,128]{1,0:T(8,128)S(1)}, f32[256,128]{1,0:T(8,128)S(1)}, u32[]{:S(2)}, u32[]{:S(2)}) collective-permute-start(f32[256,128]{1,0:T(8,128)S(1)} %get-tuple-element.32), channel_id=1, source_target_pairs={{0,6},{1,7},{2,0},{3,1},{4,2},{5,3},{6,4},{7,5},{8,14},{9,15},{10,... | collective-permute-start | bytes 393224 | tf_op jit(solution)/shard_map/ppermute | solution.py:345
  103.0 1.6 %shard_map.51.near = f32[1536,128]{1,0:T(8,128)S(1)} custom-call(s32[3]{0:T(128)S(1)} %pad_add_fusion.where.after_ref, s32[136]{0:T(256)S(1)} %shard_map.43.tab, bf16[48,128,256]{2,1,0:T(8,128)(2,1)S(1)} %shard_map.45.ls, bf16[32,256,128]{2,1,0:T(8,128)(2,1)S(1)} %shard_map.47.rs, f32[256,128]{1,0:T(8,128)S(1)} %get-tuple-element.31.after_ref), custom_call_target="tpu_custom_call" | custom-call | flops 402653184 | bytes 3145728 | tf_op jit(solution)/shard_map/pallas_call | solution.py:242
  104.6 0.6 collective-permute-done.10.half
  105.2 5.3 %collective-permute-start.11 = (f32[512,128]{1,0:T(8,128)S(1)}, f32[512,128]{1,0:T(8,128)S(1)}, u32[]{:S(2)}, u32[]{:S(2)}) collective-permute-start(f32[512,128]{1,0:T(8,128)S(1)} %shard_map.52.after_ref), channel_id=1, source_target_pairs={{0,2},{1,3},{2,4},{3,5},{4,6},{5,7},{6,0},{7,1},{8,10},{9,11},{10,... | collective-permute-start | bytes 786440 | tf_op jit(solution)/shard_map/ppermute | solution.py:345
  110.6 4.5 %collective-permute-done.12.half = f32[256,128]{1,0:T(8,128)S(1)} collective-permute-done((f32[256,128]{1,0:T(8,128)S(1)}, f32[256,128]{1,0:T(8,128)S(1)}, u32[]{:S(2)}, u32[]{:S(2)}) %collective-permute-start.12) | collective-permute-done | bytes 131104 | tf_op jit(solution)/shard_map/ppermute | solution.py:345
  115.0 0.1 shard_map.54
  115.1 1.9 %collective-permute-start.13 = (f32[512,128]{1,0:T(8,128)S(1)}, f32[512,128]{1,0:T(8,128)S(1)}, u32[]{:S(2)}, u32[]{:S(2)}) collective-permute-start(f32[512,128]{1,0:T(8,128)S(1)} %shard_map.54), channel_id=1, source_target_pairs={{0,6},{1,7},{2,0},{3,1},{4,2},{5,3},{6,4},{7,5},{8,14},{9,15},{10,... | collective-permute-start | bytes 786440 | tf_op jit(solution)/shard_map/ppermute | solution.py:345
  117.0 0.1 shard_map.53.part
  117.1 15.8 %collective-permute-done.13.d = f32[512,128]{1,0:T(8,128)S(1)} collective-permute-done((f32[512,128]{1,0:T(8,128)S(1)}, f32[512,128]{1,0:T(8,128)S(1)}, u32[]{:S(2)}, u32[]{:S(2)}) %collective-permute-start.13) | collective-permute-done | bytes 262176 | tf_op jit(solution)/shard_map/ppermute | solution.py:345
  132.9 0.9 shard_map.55
  (13 shorter events, 0.1 us)
Async XLA Ops:
  0.0 1.0 copy-start.2
  1.0 29.5 %copy-start.3 = (s32[3,512]{1,0:T(4,128)S(1)}, s32[3,512]{1,0:T(4,128)}, u32[]{:S(2)}) copy-start(s32[3,512]{1,0:T(4,128)} %t_ref.1) | copy-start | bytes 18436
  2.2 36.4 %all-to-all-start = ((f32[3,256,256]{2,1,0:T(8,128)}), f32[3,256,256]{2,1,0:T(8,128)}, u32[]{:S(2)}, u32[]{:S(2)}) async-start(f32[3,256,256]{2,1,0:T(8,128)} %get-tuple-element.19), calls=%async_computation | async-start | bytes 1572864 | tf_op jit(solution)/shard_map/all_to_all | solution.py:325
  14.9 20.6 %collective-permute-start.2 = (f32[256,256]{1,0:T(8,128)}, f32[256,256]{1,0:T(8,128)}, u32[]{:S(2)}, u32[]{:S(2)}) collective-permute-start(f32[256,256]{1,0:T(8,128)} %get-tuple-element.20.part), channel_id=1, source_target_pairs={{0,8},{8,16},{16,24},{24,0},{32,40},{40,48},{48,56},{56,32},{64,72... | collective-permute-start | bytes 786440 | tf_op jit(solution)/shard_map/ppermute | solution.py:333
  18.0 18.5 %collective-permute-start.1 = (f32[256,256]{1,0:T(8,128)}, f32[256,256]{1,0:T(8,128)}, u32[]{:S(2)}, u32[]{:S(2)}) collective-permute-start(f32[256,256]{1,0:T(8,128)} %get-tuple-element.20.part), channel_id=1, source_target_pairs={{0,16},{8,24},{16,0},{24,8},{32,48},{40,56},{48,32},{56,40},{64,80... | collective-permute-start | bytes 786440 | tf_op jit(solution)/shard_map/ppermute | solution.py:333
  20.8 16.8 %collective-permute-start = (f32[256,256]{1,0:T(8,128)}, f32[256,256]{1,0:T(8,128)}, u32[]{:S(2)}, u32[]{:S(2)}) collective-permute-start(f32[256,256]{1,0:T(8,128)} %get-tuple-element.20.part), channel_id=1, source_target_pairs={{0,24},{8,0},{16,8},{24,16},{32,56},{40,32},{48,40},{56,48},{64,88... | collective-permute-start | bytes 786440 | tf_op jit(solution)/shard_map/ppermute | solution.py:333
  24.5 1.0 copy-start.1
  25.7 12.8 %collective-permute-start.3 = (f32[256,256]{1,0:T(8,128)S(1)}, f32[256,256]{1,0:T(8,128)}, u32[]{:S(2)}, u32[]{:S(2)}) collective-permute-start(f32[256,256]{1,0:T(8,128)S(1)} %shard_map.42.r), channel_id=1, source_target_pairs={{0,96},{96,0},{192,288},{288,192},{384,480},{480,384},{576,672},{6... | collective-permute-start | bytes 786440 | tf_op jit(solution)/shard_map/ppermute | solution.py:341
  39.8 1.3 copy-start
  41.1 29.2 %all-to-all-start.1 = ((f32[4,512,256]{2,1,0:T(8,128)}), f32[4,512,256]{2,1,0:T(8,128)}, u32[]{:S(2)}, u32[]{:S(2)}) async-start(f32[4,512,256]{2,1,0:T(8,128)} %copy-done), calls=%async_computation.1 | async-start | bytes 4194304 | tf_op jit(solution)/shard_map/all_to_all | solution.py:325
  46.7 25.5 %collective-permute-start.4 = (f32[256,256]{1,0:T(8,128)S(1)}, f32[256,256]{1,0:T(8,128)}, u32[]{:S(2)}, u32[]{:S(2)}) collective-permute-start(f32[256,256]{1,0:T(8,128)S(1)} %shard_map.42.r), channel_id=1, source_target_pairs={{0,192},{96,288},{192,384},{288,480},{384,576},{480,672},{576,0},{... | collective-permute-start | bytes 786440 | tf_op jit(solution)/shard_map/ppermute | solution.py:337
  51.2 22.4 %collective-permute-start.5 = (f32[256,256]{1,0:T(8,128)S(1)}, f32[256,256]{1,0:T(8,128)}, u32[]{:S(2)}, u32[]{:S(2)}) collective-permute-start(f32[256,256]{1,0:T(8,128)S(1)} %shard_map.42.r), channel_id=1, source_target_pairs={{0,384},{96,480},{192,576},{288,672},{384,0},{480,96},{576,192},{6... | collective-permute-start | bytes 786440 | tf_op jit(solution)/shard_map/ppermute | solution.py:337
  57.4 21.8 %collective-permute-start.6 = (f32[256,256]{1,0:T(8,128)S(1)}, f32[256,256]{1,0:T(8,128)}, u32[]{:S(2)}, u32[]{:S(2)}) collective-permute-start(f32[256,256]{1,0:T(8,128)S(1)} %shard_map.42.r), channel_id=1, source_target_pairs={{0,576},{96,672},{192,0},{288,96},{384,192},{480,288},{576,384},{6... | collective-permute-start | bytes 786440 | tf_op jit(solution)/shard_map/ppermute | solution.py:337
  80.3 4.3 %collective-permute-start.7 = (f32[3,256,256]{2,1,0:T(8,128)S(1)}, f32[3,256,256]{2,1,0:T(8,128)S(1)}, u32[]{:S(2)}, u32[]{:S(2)}) collective-permute-start(f32[3,256,256]{2,1,0:T(8,128)S(1)} %pad_maximum_fusion), channel_id=1, source_target_pairs={{0,96},{96,0},{192,288},{288,192},{384,480},{480,384},{576,672},{6... | collective-permute-start | bytes 2359304 | tf_op jit(solution)/shard_map/ppermute | solution.py:341
  86.7 18.5 %collective-permute-start.8 = (f32[1024,128]{1,0:T(8,128)S(1)}, f32[1024,128]{1,0:T(8,128)S(1)}, u32[]{:S(2)}, u32[]{:S(2)}) collective-permute-start(f32[1024,128]{1,0:T(8,128)S(1)} %shard_map.48.after_ref), channel_id=1, source_target_pairs={{0,1},{1,2},{2,3},{3,4},{4,5},{5,6},{6,7},{7,0},{8,9},{9,10},{10,1... | collective-permute-start | bytes 1572872 | tf_op jit(solution)/shard_map/ppermute | solution.py:345
  91.3 23.8 %collective-permute-start.9 = (f32[1024,128]{1,0:T(8,128)S(1)}, f32[1024,128]{1,0:T(8,128)S(1)}, u32[]{:S(2)}, u32[]{:S(2)}) collective-permute-start(f32[1024,128]{1,0:T(8,128)S(1)} %shard_map.49.after_ref), channel_id=1, source_target_pairs={{0,7},{1,0},{2,1},{3,2},{4,3},{5,4},{6,5},{7,6},{8,15},{9,8},{10,9... | collective-permute-start | bytes 1572872 | tf_op jit(solution)/shard_map/ppermute | solution.py:345
  94.4 10.8 %collective-permute-start.10 = (f32[256,128]{1,0:T(8,128)S(1)}, f32[256,128]{1,0:T(8,128)S(1)}, u32[]{:S(2)}, u32[]{:S(2)}) collective-permute-start(f32[256,128]{1,0:T(8,128)S(1)} %get-tuple-element.31.after_ref), channel_id=1, source_target_pairs={{0,2},{1,3},{2,4},{3,5},{4,6},{5,7},{6,0},{7,1},{8,10},{9,11},{10,... | collective-permute-start | bytes 393224 | tf_op jit(solution)/shard_map/ppermute | solution.py:345
  101.0 14.0 %collective-permute-start.12 = (f32[256,128]{1,0:T(8,128)S(1)}, f32[256,128]{1,0:T(8,128)S(1)}, u32[]{:S(2)}, u32[]{:S(2)}) collective-permute-start(f32[256,128]{1,0:T(8,128)S(1)} %get-tuple-element.32), channel_id=1, source_target_pairs={{0,6},{1,7},{2,0},{3,1},{4,2},{5,3},{6,4},{7,5},{8,14},{9,15},{10,... | collective-permute-start | bytes 393224 | tf_op jit(solution)/shard_map/ppermute | solution.py:345
  105.2 11.8 %collective-permute-start.11 = (f32[512,128]{1,0:T(8,128)S(1)}, f32[512,128]{1,0:T(8,128)S(1)}, u32[]{:S(2)}, u32[]{:S(2)}) collective-permute-start(f32[512,128]{1,0:T(8,128)S(1)} %shard_map.52.after_ref), channel_id=1, source_target_pairs={{0,2},{1,3},{2,4},{3,5},{4,6},{5,7},{6,0},{7,1},{8,10},{9,11},{10,... | collective-permute-start | bytes 786440 | tf_op jit(solution)/shard_map/ppermute | solution.py:345
  115.1 17.8 %collective-permute-start.13 = (f32[512,128]{1,0:T(8,128)S(1)}, f32[512,128]{1,0:T(8,128)S(1)}, u32[]{:S(2)}, u32[]{:S(2)}) collective-permute-start(f32[512,128]{1,0:T(8,128)S(1)} %shard_map.54), channel_id=1, source_target_pairs={{0,6},{1,7},{2,0},{3,1},{4,2},{5,3},{6,4},{7,5},{8,14},{9,15},{10,... | collective-permute-start | bytes 786440 | tf_op jit(solution)/shard_map/ppermute | solution.py:345

commit v4 on v3

--- a/solution.py
+++ b/solution.py
@@ -194,18 +194,21 @@
     )(where, ls, xs)
 
 
-def first_right_kernel(where, r, sibling, r1, r2, r3, rs):
+def first_right_kernel(where, r, sibling, r1, r2, s1, s2, rs):
     z, core = where[2] >> 1, where[2] & 1
+    prep_right(r, rs, z * 2 + core)
     prep_right(sibling, rs, z * 2 + 1 - core)
-    for k, ref in enumerate((r, r1, r2, r3)):
-        prep_right(ref, rs, ((z + 4 - k) & 3) * 2 + core)
+    prep_right(r1, rs, (z ^ 1) * 2 + core)
+    prep_right(r2, rs, (z ^ 2) * 2 + core)
+    prep_right(s1, rs, (z ^ 1) * 2 + 1 - core)
+    prep_right(s2, rs, (z ^ 2) * 2 + 1 - core)
 
 
 def first_right(where, *parts):
     return pl.pallas_call(
         first_right_kernel,
         out_shape=RIGHT,
-        in_specs=[SM] + [VM] * 5,
+        in_specs=[SM] + [VM] * 6,
         out_specs=VM,
         compiler_params=params(),
         cost_estimate=cost(0, 2**22),
@@ -216,22 +219,22 @@
     return ((where[0] + 8 + k) & 7) * SHARE
 
 
-def last_right_kernel(where, rs_in, s3, rs):
+def last_right_kernel(where, rs_in, r3, s3, rs):
     z, core = where[2] >> 1, where[2] & 1
-    for k in range(3):
-        prep_right(s3.at[k], rs, ((z + 3 - k) & 3) * 2 + 1 - core)
-
-
-def last_right(where, rs, s4):
+    prep_right(r3, rs, (z ^ 3) * 2 + core)
+    prep_right(s3, rs, (z ^ 3) * 2 + 1 - core)
+
+
+def last_right(where, rs, r3, s3):
     return pl.pallas_call(
         last_right_kernel,
         out_shape=RIGHT,
-        in_specs=[SM, VM, VM],
+        in_specs=[SM, VM, VM, VM],
         out_specs=VM,
         input_output_aliases={1: 0},
         compiler_params=params(),
-        cost_estimate=cost(0, 2**22),
-    )(where, rs, s4)
+        cost_estimate=cost(0, 2**21),
+    )(where, rs, r3, s3)
 
 
 def shares(where, tab, ls, rs, offsets, after):
@@ -333,8 +336,8 @@
     return lax.ppermute(x, "col", [(z * 4 + c, z * 4 + (c + k) % 4) for z in range(3) for c in range(4)])
 
 
-def along_z(x, k):
-    return lax.ppermute(x, "row", [(z * 2 + c, (z + k) % 4 * 2 + c) for z in range(4) for c in range(2)])
+def swap_z(x, k):
+    return lax.ppermute(x, "row", [(i, i ^ (2 * k)) for i in range(8)])
 
 
 def swap_core(x):
@@ -358,11 +361,13 @@
         ls = split_one(where, k, along_x(l, k), ls)
     zs, ls, sibling, tab, r, where = lax.optimization_barrier((zs, ls, sibling, tab, r, where))
     xs = to_group(spread(where, zs), "col", X_GROUPS)
-    rk = [along_z(r, k) for k in (1, 2, 3)]
+    r2, r1 = swap_z(r, 2), swap_z(r, 1)
+    r3 = swap_z(r2, 1)
+    s1, s2 = swap_core(r1), swap_core(r2)
     ls = split_others(where, ls, xs)
-    rk, ls = lax.optimization_barrier((rk, ls))
-    s3 = swap_core(jnp.stack(rk))
-    rs = last_right(where, first_right(where, r, sibling, *rk), s3)
+    r3, ls = lax.optimization_barrier((r3, ls))
+    rs = first_right(where, r, sibling, r1, r2, s1, s2)
+    rs = last_right(where, rs, r3, swap_core(r3))
     p3 = shares(where, tab, ls, rs, (3, 1), where)
     m3 = shares(where, tab, ls, rs, (-3, -1), p3)
     f0, f1 = far(where, tab, ls, rs, m3)

time: 135 us -> 133 us (0.985)
  the two profiles are of different devices: /device:TPU:83 before, /device:TPU:209 now
where the time goes in v4:
time: 133 us; the launch traced here: 132 us
  starting transfers between devices  63.9 us (48%)
  waiting for transfers between devices  42 us (32%)
  Pallas kernels  22.4 us (17%)
  local copies, waits for them, and re-layouts  3.38 us (3%)
    ppermute x6, waiting for transfers between devices, along_depth(): lax.ppermute(x, 'depth', [(i, (i + k) % LAYERS) for i in range(LAYERS)])  21.8 us
    ppermute x6, starting transfers between devices, along_depth(): lax.ppermute(x, 'depth', [(i, (i + k) % LAYERS) for i in range(LAYERS)])  20.6 us
    all_to_all x2, starting transfers between devices, to_group(): return lax.all_to_all(x, axis, 0, 0, axis_index_groups=groups)  15.4 us
    ppermute x4, starting transfers between devices, swap_core(): return lax.ppermute(x, 'row', [(i, i ^ 1) for i in range(8)])  11.7 us
    all_to_all x2, waiting for transfers between devices, to_group(): return lax.all_to_all(x, axis, 0, 0, axis_index_groups=groups)  10.7 us
    ppermute x3, starting transfers between devices, along_x(): lax.ppermute(x, 'col', [(z * 4 + c, z * 4 + (c + k) % 4) for z in range(3...  10.5 us
    ppermute x3, waiting for transfers between devices, swap_z(): return lax.ppermute(x, 'row', [(i, i ^ 2 * k) for i in range(8)])  9.58 us
    ppermute x3, starting transfers between devices, swap_z(): return lax.ppermute(x, 'row', [(i, i ^ 2 * k) for i in range(8)])  5.75 us
  transfers between devices with their start and end apart: 18, of which 6 were waited for; matrix products, arithmetic and copies ran while one was open for 0% of the time, Pallas kernels for 13%

profile of v4, /device:TPU:209, one launch (start us, length us, event | category | flops | bytes accessed | tf_op | source)
XLA Modules:
  0.0 132.2 jit_solution(470250807913058329)
XLA Ops:
  0.0 1.0 copy-done.2
  1.0 1.1 shard_map.37
  2.2 10.9 %all-to-all-start = ((f32[3,256,256]{2,1,0:T(8,128)}), f32[3,256,256]{2,1,0:T(8,128)}, u32[]{:S(2)}, u32[]{:S(2)}) async-start(f32[3,256,256]{2,1,0:T(8,128)} %get-tuple-element.17), calls=%async_computation | async-start | bytes 1572864 | tf_op jit(solution)/shard_map/all_to_all | solution.py:328
  13.1 3.1 %collective-permute-start.2 = (f32[256,256]{1,0:T(8,128)}, f32[256,256]{1,0:T(8,128)}, u32[]{:S(2)}, u32[]{:S(2)}) collective-permute-start(f32[256,256]{1,0:T(8,128)} %get-tuple-element.18.part), channel_id=1, source_target_pairs={{0,8},{8,16},{16,24},{24,0},{32,40},{40,48},{48,56},{56,32},{64,72... | collective-permute-start | bytes 786440 | tf_op jit(solution)/shard_map/ppermute | solution.py:336
  16.2 4.4 %collective-permute-start.1 = (f32[256,256]{1,0:T(8,128)}, f32[256,256]{1,0:T(8,128)}, u32[]{:S(2)}, u32[]{:S(2)}) collective-permute-start(f32[256,256]{1,0:T(8,128)} %get-tuple-element.18.part), channel_id=1, source_target_pairs={{0,16},{8,24},{16,0},{24,8},{32,48},{40,56},{48,32},{56,40},{64,80... | collective-permute-start | bytes 786440 | tf_op jit(solution)/shard_map/ppermute | solution.py:336
  20.6 3.1 %collective-permute-start = (f32[256,256]{1,0:T(8,128)}, f32[256,256]{1,0:T(8,128)}, u32[]{:S(2)}, u32[]{:S(2)}) collective-permute-start(f32[256,256]{1,0:T(8,128)} %get-tuple-element.18.part), channel_id=1, source_target_pairs={{0,24},{8,0},{16,8},{24,16},{32,56},{40,32},{48,40},{56,48},{64,88... | collective-permute-start | bytes 786440 | tf_op jit(solution)/shard_map/ppermute | solution.py:336
  23.6 0.0 copy-start.1
  23.7 1.0 copy-done.1
  24.7 0.1 shard_map.42.r
  24.8 3.7 %collective-permute-start.3 = (f32[256,256]{1,0:T(8,128)S(1)}, f32[256,256]{1,0:T(8,128)}, u32[]{:S(2)}, u32[]{:S(2)}) collective-permute-start(f32[256,256]{1,0:T(8,128)S(1)} %shard_map.42.r), channel_id=1, source_target_pairs={{0,96},{96,0},{192,288},{288,192},{384,480},{480,384},{576,672},{6... | collective-permute-start | bytes 786440 | tf_op jit(solution)/shard_map/ppermute | solution.py:344
  28.6 0.1 pad_add_fusion.where.after_ref
  28.6 1.0 shard_map.38.rest_0_
  29.6 4.9 %shard_map.43.tab = s32[136]{0:T(256)S(1)} custom-call(s32[3,512]{1,0:T(4,128)S(1)} %copy-done.3), custom_call_target="tpu_custom_call" | custom-call | bytes 8388608 | tf_op jit(solution)/shard_map/pallas_call | solution.py:86
  34.6 0.0 collective-permute-done.2.part
  34.6 1.0 shard_map.39.rest_0_
  35.6 1.0 shard_map.40.rest_0_
  36.6 1.0 shard_map.41.ls_in
  37.6 4.7 %all-to-all-done.zs = f32[3,256,256]{2,1,0:T(8,128)} async-done(((f32[3,256,256]{2,1,0:T(8,128)}), f32[3,256,256]{2,1,0:T(8,128)}, u32[]{:S(2)}, u32[]{:S(2)}) %all-to-all-start) | async-done | bytes 786464 | tf_op jit(solution)/shard_map/all_to_all | solution.py:328
  42.4 1.3 shard_map.44
  43.7 1.3 copy-done
  45.0 4.5 %all-to-all-start.1 = ((f32[4,512,256]{2,1,0:T(8,128)}), f32[4,512,256]{2,1,0:T(8,128)}, u32[]{:S(2)}, u32[]{:S(2)}) async-start(f32[4,512,256]{2,1,0:T(8,128)} %copy-done), calls=%async_computation.1 | async-start | bytes 4194304 | tf_op jit(solution)/shard_map/all_to_all | solution.py:328
  49.4 1.9 %collective-permute-start.4 = (f32[256,256]{1,0:T(8,128)S(1)}, f32[256,256]{1,0:T(8,128)}, u32[]{:S(2)}, u32[]{:S(2)}) collective-permute-start(f32[256,256]{1,0:T(8,128)S(1)} %shard_map.42.r), channel_id=1, source_target_pairs={{0,384},{96,480},{192,576},{288,672},{384,0},{480,96},{576,192},{6... | collective-permute-start | bytes 786440 | tf_op jit(solution)/shard_map/ppermute | solution.py:340
  51.4 1.9 %collective-permute-start.6 = (f32[256,256]{1,0:T(8,128)S(1)}, f32[256,256]{1,0:T(8,128)}, u32[]{:S(2)}, u32[]{:S(2)}) collective-permute-start(f32[256,256]{1,0:T(8,128)S(1)} %shard_map.42.r), channel_id=1, source_target_pairs={{0,192},{96,288},{192,0},{288,96},{384,576},{480,672},{576,384},{6... | collective-permute-start | bytes 786440 | tf_op jit(solution)/shard_map/ppermute | solution.py:340
  53.3 9.6 %collective-permute-done.4.r2 = f32[256,256]{1,0:T(8,128)} collective-permute-done((f32[256,256]{1,0:T(8,128)S(1)}, f32[256,256]{1,0:T(8,128)}, u32[]{:S(2)}, u32[]{:S(2)}) %collective-permute-start.4) | collective-permute-done | bytes 262176 | tf_op jit(solution)/shard_map/ppermute | solution.py:340
  62.9 1.9 %collective-permute-start.5 = (f32[256,256]{1,0:T(8,128)}, f32[256,256]{1,0:T(8,128)}, u32[]{:S(2)}, u32[]{:S(2)}) collective-permute-start(f32[256,256]{1,0:T(8,128)} %collective-permute-done.4.r2), channel_id=1, source_target_pairs={{0,192},{96,288},{192,0},{288,96},{384,576},{480,672},{576,384},{6... | collective-permute-start | bytes 786440 | tf_op jit(solution)/shard_map/ppermute | solution.py:340
  64.8 2.5 %collective-permute-start.8 = (f32[256,256]{1,0:T(8,128)}, f32[256,256]{1,0:T(8,128)}, u32[]{:S(2)}, u32[]{:S(2)}) collective-permute-start(f32[256,256]{1,0:T(8,128)} %collective-permute-done.4.r2), channel_id=1, source_target_pairs={{0,96},{96,0},{192,288},{288,192},{384,480},{480,384},{576,672},{6... | collective-permute-start | bytes 786440 | tf_op jit(solution)/shard_map/ppermute | solution.py:344
  67.3 2.2 %collective-permute-start.7 = (f32[256,256]{1,0:T(8,128)}, f32[256,256]{1,0:T(8,128)}, u32[]{:S(2)}, u32[]{:S(2)}) collective-permute-start(f32[256,256]{1,0:T(8,128)} %collective-permute-done.6.r1), channel_id=1, source_target_pairs={{0,96},{96,0},{192,288},{288,192},{384,480},{480,384},{576,672},{6... | collective-permute-start | bytes 786440 | tf_op jit(solution)/shard_map/ppermute | solution.py:344
  69.5 5.9 %all-to-all-done.1.xs = f32[4,512,256]{2,1,0:T(8,128)} async-done(((f32[4,512,256]{2,1,0:T(8,128)}), f32[4,512,256]{2,1,0:T(8,128)}, u32[]{:S(2)}, u32[]{:S(2)}) %all-to-all-start.1) | async-done | bytes 2097184 | tf_op jit(solution)/shard_map/all_to_all | solution.py:328
  75.4 1.8 %shard_map.45.ls = bf16[48,128,256]{2,1,0:T(8,128)(2,1)S(1)} custom-call(s32[3]{0:T(128)S(1)} %pad_add_fusion.where.after_ref, bf16[48,128,256]{2,1,0:T(8,128)(2,1)S(1)} %shard_map.41.ls_in, f32[4,512,256]{2,1,0:T(8,128)} %all-to-all-done.1.xs), custom_call_target="tpu_custom_call", output_to_operand_aliasing={{}: (1, {})} | custom-call | bytes 4194304 | tf_op jit(solution)/shard_map/pallas_call | solution.py:186
  77.3 3.2 %collective-permute-start.9 = (f32[256,256]{1,0:T(8,128)}, f32[256,256]{1,0:T(8,128)S(1)}, u32[]{:S(2)}, u32[]{:S(2)}) collective-permute-start(f32[256,256]{1,0:T(8,128)} %collective-permute-done.5.r3), channel_id=1, source_target_pairs={{0,96},{96,0},{192,288},{288,192},{384,480},{480,384},{576,672},{6... | collective-permute-start | bytes 786440 | tf_op jit(solution)/shard_map/ppermute | solution.py:344
  80.6 1.7 %shard_map.46.rs_in = bf16[32,256,128]{2,1,0:T(8,128)(2,1)S(1)} custom-call(s32[3]{0:T(128)S(1)} %pad_add_fusion.where.after_ref, f32[256,256]{1,0:T(8,128)S(1)} %shard_map.42.r, f32[256,256]{1,0:T(8,128)} %collective-permute-done.3.sibling, f32[256,256]{1,0:T(8,128)} %collective-permute-done.6.r1, f32[256,256]{1,0:T(8,128)} %collective-permute-done.4.r2, ...), custom_call_target="tpu_custom_call" | custom-call | bytes 4194304 | tf_op jit(solution)/shard_map/pallas_call | solution.py:208
  82.2 1.1 shard_map.47.rs
  83.3 1.3 %shard_map.48.after_ref = f32[1024,128]{1,0:T(8,128)S(1)} custom-call(s32[3]{0:T(128)S(1)} %pad_add_fusion.where.after_ref, s32[136]{0:T(256)S(1)} %shard_map.43.tab, bf16[48,128,256]{2,1,0:T(8,128)(2,1)S(1)} %shard_map.45.ls, bf16[32,256,128]{2,1,0:T(8,128)(2,1)S(1)} %shard_map.47.rs, s32[3]{0:T(128)S(1)} %pad_add_fusion.where.after_ref), custom_call_target="tpu_custom_call" | custom-call | flops 268435456 | bytes 2097152 | tf_op jit(solution)/shard_map/pallas_call | solution.py:245
  84.7 3.2 %collective-permute-start.10 = (f32[1024,128]{1,0:T(8,128)S(1)}, f32[1024,128]{1,0:T(8,128)S(1)}, u32[]{:S(2)}, u32[]{:S(2)}) collective-permute-start(f32[1024,128]{1,0:T(8,128)S(1)} %shard_map.48.after_ref), channel_id=1, source_target_pairs={{0,1},{1,2},{2,3},{3,4},{4,5},{5,6},{6,7},{7,0},{8,9},{9,10},{10,1... | collective-permute-start | bytes 1572872 | tf_op jit(solution)/shard_map/ppermute | solution.py:348
  87.9 1.3 %shard_map.49.after_ref = f32[1024,128]{1,0:T(8,128)S(1)} custom-call(s32[3]{0:T(128)S(1)} %pad_add_fusion.where.after_ref, s32[136]{0:T(256)S(1)} %shard_map.43.tab, bf16[48,128,256]{2,1,0:T(8,128)(2,1)S(1)} %shard_map.45.ls, bf16[32,256,128]{2,1,0:T(8,128)(2,1)S(1)} %shard_map.47.rs, f32[1024,128]{1,0:T(8,128)S(1)} %shard_map.48.after_ref), custom_call_target="tpu_custom_call" | custom-call | flops 268435456 | bytes 2097152 | tf_op jit(solution)/shard_map/pallas_call | solution.py:245
  89.2 2.1 %collective-permute-start.11 = (f32[1024,128]{1,0:T(8,128)S(1)}, f32[1024,128]{1,0:T(8,128)S(1)}, u32[]{:S(2)}, u32[]{:S(2)}) collective-permute-start(f32[1024,128]{1,0:T(8,128)S(1)} %shard_map.49.after_ref), channel_id=1, source_target_pairs={{0,7},{1,0},{2,1},{3,2},{4,3},{5,4},{6,5},{7,6},{8,15},{9,8},{10,9... | collective-permute-start | bytes 1572872 | tf_op jit(solution)/shard_map/ppermute | solution.py:348
  91.3 1.1 shard_map.50
  92.4 6.6 %collective-permute-start.12 = (f32[256,128]{1,0:T(8,128)S(1)}, f32[256,128]{1,0:T(8,128)S(1)}, u32[]{:S(2)}, u32[]{:S(2)}) collective-permute-start(f32[256,128]{1,0:T(8,128)S(1)} %get-tuple-element.27.after_ref), channel_id=1, source_target_pairs={{0,2},{1,3},{2,4},{3,5},{4,6},{5,7},{6,0},{7,1},{8,10},{9,11},{10,... | collective-permute-start | bytes 393224 | tf_op jit(solution)/shard_map/ppermute | solution.py:348
  99.0 1.9 %collective-permute-start.14 = (f32[256,128]{1,0:T(8,128)S(1)}, f32[256,128]{1,0:T(8,128)S(1)}, u32[]{:S(2)}, u32[]{:S(2)}) collective-permute-start(f32[256,128]{1,0:T(8,128)S(1)} %get-tuple-element.28), channel_id=1, source_target_pairs={{0,6},{1,7},{2,0},{3,1},{4,2},{5,3},{6,4},{7,5},{8,14},{9,15},{10,... | collective-permute-start | bytes 393224 | tf_op jit(solution)/shard_map/ppermute | solution.py:348
  100.9 1.6 %shard_map.51.near = f32[1536,128]{1,0:T(8,128)S(1)} custom-call(s32[3]{0:T(128)S(1)} %pad_add_fusion.where.after_ref, s32[136]{0:T(256)S(1)} %shard_map.43.tab, bf16[48,128,256]{2,1,0:T(8,128)(2,1)S(1)} %shard_map.45.ls, bf16[32,256,128]{2,1,0:T(8,128)(2,1)S(1)} %shard_map.47.rs, f32[256,128]{1,0:T(8,128)S(1)} %get-tuple-element.27.after_ref), custom_call_target="tpu_custom_call" | custom-call | flops 402653184 | bytes 3145728 | tf_op jit(solution)/shard_map/pallas_call | solution.py:245
  102.5 2.0 %collective-permute-done.12.half = f32[256,128]{1,0:T(8,128)S(1)} collective-permute-done((f32[256,128]{1,0:T(8,128)S(1)}, f32[256,128]{1,0:T(8,128)S(1)}, u32[]{:S(2)}, u32[]{:S(2)}) %collective-permute-start.12) | collective-permute-done | bytes 131104 | tf_op jit(solution)/shard_map/ppermute | solution.py:348
  104.6 4.8 %collective-permute-start.13 = (f32[512,128]{1,0:T(8,128)S(1)}, f32[512,128]{1,0:T(8,128)S(1)}, u32[]{:S(2)}, u32[]{:S(2)}) collective-permute-start(f32[512,128]{1,0:T(8,128)S(1)} %shard_map.52.after_ref), channel_id=1, source_target_pairs={{0,2},{1,3},{2,4},{3,5},{4,6},{5,7},{6,0},{7,1},{8,10},{9,11},{10,... | collective-permute-start | bytes 786440 | tf_op jit(solution)/shard_map/ppermute | solution.py:348
  109.4 4.0 %collective-permute-done.14.half = f32[256,128]{1,0:T(8,128)S(1)} collective-permute-done((f32[256,128]{1,0:T(8,128)S(1)}, f32[256,128]{1,0:T(8,128)S(1)}, u32[]{:S(2)}, u32[]{:S(2)}) %collective-permute-start.14) | collective-permute-done | bytes 131104 | tf_op jit(solution)/shard_map/ppermute | solution.py:348
  113.4 0.1 shard_map.54
  113.4 1.9 %collective-permute-start.15 = (f32[512,128]{1,0:T(8,128)S(1)}, f32[512,128]{1,0:T(8,128)S(1)}, u32[]{:S(2)}, u32[]{:S(2)}) collective-permute-start(f32[512,128]{1,0:T(8,128)S(1)} %shard_map.54), channel_id=1, source_target_pairs={{0,6},{1,7},{2,0},{3,1},{4,2},{5,3},{6,4},{7,5},{8,14},{9,15},{10,... | collective-permute-start | bytes 786440 | tf_op jit(solution)/shard_map/ppermute | solution.py:348
  115.4 0.1 shard_map.53.part
  115.4 15.8 %collective-permute-done.15.d = f32[512,128]{1,0:T(8,128)S(1)} collective-permute-done((f32[512,128]{1,0:T(8,128)S(1)}, f32[512,128]{1,0:T(8,128)S(1)}, u32[]{:S(2)}, u32[]{:S(2)}) %collective-permute-start.15) | collective-permute-done | bytes 262176 | tf_op jit(solution)/shard_map/ppermute | solution.py:348
  131.2 0.9 shard_map.55
  (16 shorter events, 0.1 us)
Async XLA Ops:
  0.0 1.0 copy-start.2
  1.0 28.6 %copy-start.3 = (s32[3,512]{1,0:T(4,128)S(1)}, s32[3,512]{1,0:T(4,128)}, u32[]{:S(2)}) copy-start(s32[3,512]{1,0:T(4,128)} %t_ref.1) | copy-start | bytes 18436
  2.2 40.2 %all-to-all-start = ((f32[3,256,256]{2,1,0:T(8,128)}), f32[3,256,256]{2,1,0:T(8,128)}, u32[]{:S(2)}, u32[]{:S(2)}) async-start(f32[3,256,256]{2,1,0:T(8,128)} %get-tuple-element.17), calls=%async_computation | async-start | bytes 1572864 | tf_op jit(solution)/shard_map/all_to_all | solution.py:328
  13.1 21.5 %collective-permute-start.2 = (f32[256,256]{1,0:T(8,128)}, f32[256,256]{1,0:T(8,128)}, u32[]{:S(2)}, u32[]{:S(2)}) collective-permute-start(f32[256,256]{1,0:T(8,128)} %get-tuple-element.18.part), channel_id=1, source_target_pairs={{0,8},{8,16},{16,24},{24,0},{32,40},{40,48},{48,56},{56,32},{64,72... | collective-permute-start | bytes 786440 | tf_op jit(solution)/shard_map/ppermute | solution.py:336
  16.2 19.4 %collective-permute-start.1 = (f32[256,256]{1,0:T(8,128)}, f32[256,256]{1,0:T(8,128)}, u32[]{:S(2)}, u32[]{:S(2)}) collective-permute-start(f32[256,256]{1,0:T(8,128)} %get-tuple-element.18.part), channel_id=1, source_target_pairs={{0,16},{8,24},{16,0},{24,8},{32,48},{40,56},{48,32},{56,40},{64,80... | collective-permute-start | bytes 786440 | tf_op jit(solution)/shard_map/ppermute | solution.py:336
  20.6 16.0 %collective-permute-start = (f32[256,256]{1,0:T(8,128)}, f32[256,256]{1,0:T(8,128)}, u32[]{:S(2)}, u32[]{:S(2)}) collective-permute-start(f32[256,256]{1,0:T(8,128)} %get-tuple-element.18.part), channel_id=1, source_target_pairs={{0,24},{8,0},{16,8},{24,16},{32,56},{40,32},{48,40},{56,48},{64,88... | collective-permute-start | bytes 786440 | tf_op jit(solution)/shard_map/ppermute | solution.py:336
  23.6 1.0 copy-start.1
  24.8 12.8 %collective-permute-start.3 = (f32[256,256]{1,0:T(8,128)S(1)}, f32[256,256]{1,0:T(8,128)}, u32[]{:S(2)}, u32[]{:S(2)}) collective-permute-start(f32[256,256]{1,0:T(8,128)S(1)} %shard_map.42.r), channel_id=1, source_target_pairs={{0,96},{96,0},{192,288},{288,192},{384,480},{480,384},{576,672},{6... | collective-permute-start | bytes 786440 | tf_op jit(solution)/shard_map/ppermute | solution.py:344
  43.7 1.3 copy-start
  45.0 30.5 %all-to-all-start.1 = ((f32[4,512,256]{2,1,0:T(8,128)}), f32[4,512,256]{2,1,0:T(8,128)}, u32[]{:S(2)}, u32[]{:S(2)}) async-start(f32[4,512,256]{2,1,0:T(8,128)} %copy-done), calls=%async_computation.1 | async-start | bytes 4194304 | tf_op jit(solution)/shard_map/all_to_all | solution.py:328
  49.4 13.4 %collective-permute-start.4 = (f32[256,256]{1,0:T(8,128)S(1)}, f32[256,256]{1,0:T(8,128)}, u32[]{:S(2)}, u32[]{:S(2)}) collective-permute-start(f32[256,256]{1,0:T(8,128)S(1)} %shard_map.42.r), channel_id=1, source_target_pairs={{0,384},{96,480},{192,576},{288,672},{384,0},{480,96},{576,192},{6... | collective-permute-start | bytes 786440 | tf_op jit(solution)/shard_map/ppermute | solution.py:340
  51.4 15.9 %collective-permute-start.6 = (f32[256,256]{1,0:T(8,128)S(1)}, f32[256,256]{1,0:T(8,128)}, u32[]{:S(2)}, u32[]{:S(2)}) collective-permute-start(f32[256,256]{1,0:T(8,128)S(1)} %shard_map.42.r), channel_id=1, source_target_pairs={{0,192},{96,288},{192,0},{288,96},{384,576},{480,672},{576,384},{6... | collective-permute-start | bytes 786440 | tf_op jit(solution)/shard_map/ppermute | solution.py:340
  62.9 14.4 %collective-permute-start.5 = (f32[256,256]{1,0:T(8,128)}, f32[256,256]{1,0:T(8,128)}, u32[]{:S(2)}, u32[]{:S(2)}) collective-permute-start(f32[256,256]{1,0:T(8,128)} %collective-permute-done.4.r2), channel_id=1, source_target_pairs={{0,192},{96,288},{192,0},{288,96},{384,576},{480,672},{576,384},{6... | collective-permute-start | bytes 786440 | tf_op jit(solution)/shard_map/ppermute | solution.py:340
  64.8 15.8 %collective-permute-start.8 = (f32[256,256]{1,0:T(8,128)}, f32[256,256]{1,0:T(8,128)}, u32[]{:S(2)}, u32[]{:S(2)}) collective-permute-start(f32[256,256]{1,0:T(8,128)} %collective-permute-done.4.r2), channel_id=1, source_target_pairs={{0,96},{96,0},{192,288},{288,192},{384,480},{480,384},{576,672},{6... | collective-permute-start | bytes 786440 | tf_op jit(solution)/shard_map/ppermute | solution.py:344
  67.3 13.3 %collective-permute-start.7 = (f32[256,256]{1,0:T(8,128)}, f32[256,256]{1,0:T(8,128)}, u32[]{:S(2)}, u32[]{:S(2)}) collective-permute-start(f32[256,256]{1,0:T(8,128)} %collective-permute-done.6.r1), channel_id=1, source_target_pairs={{0,96},{96,0},{192,288},{288,192},{384,480},{480,384},{576,672},{6... | collective-permute-start | bytes 786440 | tf_op jit(solution)/shard_map/ppermute | solution.py:344
  77.3 4.9 %collective-permute-start.9 = (f32[256,256]{1,0:T(8,128)}, f32[256,256]{1,0:T(8,128)S(1)}, u32[]{:S(2)}, u32[]{:S(2)}) collective-permute-start(f32[256,256]{1,0:T(8,128)} %collective-permute-done.5.r3), channel_id=1, source_target_pairs={{0,96},{96,0},{192,288},{288,192},{384,480},{480,384},{576,672},{6... | collective-permute-start | bytes 786440 | tf_op jit(solution)/shard_map/ppermute | solution.py:344
  84.7 19.8 %collective-permute-start.10 = (f32[1024,128]{1,0:T(8,128)S(1)}, f32[1024,128]{1,0:T(8,128)S(1)}, u32[]{:S(2)}, u32[]{:S(2)}) collective-permute-start(f32[1024,128]{1,0:T(8,128)S(1)} %shard_map.48.after_ref), channel_id=1, source_target_pairs={{0,1},{1,2},{2,3},{3,4},{4,5},{5,6},{6,7},{7,0},{8,9},{9,10},{10,1... | collective-permute-start | bytes 1572872 | tf_op jit(solution)/shard_map/ppermute | solution.py:348
  89.2 24.2 %collective-permute-start.11 = (f32[1024,128]{1,0:T(8,128)S(1)}, f32[1024,128]{1,0:T(8,128)S(1)}, u32[]{:S(2)}, u32[]{:S(2)}) collective-permute-start(f32[1024,128]{1,0:T(8,128)S(1)} %shard_map.49.after_ref), channel_id=1, source_target_pairs={{0,7},{1,0},{2,1},{3,2},{4,3},{5,4},{6,5},{7,6},{8,15},{9,8},{10,9... | collective-permute-start | bytes 1572872 | tf_op jit(solution)/shard_map/ppermute | solution.py:348
  92.4 12.2 %collective-permute-start.12 = (f32[256,128]{1,0:T(8,128)S(1)}, f32[256,128]{1,0:T(8,128)S(1)}, u32[]{:S(2)}, u32[]{:S(2)}) collective-permute-start(f32[256,128]{1,0:T(8,128)S(1)} %get-tuple-element.27.after_ref), channel_id=1, source_target_pairs={{0,2},{1,3},{2,4},{3,5},{4,6},{5,7},{6,0},{7,1},{8,10},{9,11},{10,... | collective-permute-start | bytes 393224 | tf_op jit(solution)/shard_map/ppermute | solution.py:348
  99.0 14.4 %collective-permute-start.14 = (f32[256,128]{1,0:T(8,128)S(1)}, f32[256,128]{1,0:T(8,128)S(1)}, u32[]{:S(2)}, u32[]{:S(2)}) collective-permute-start(f32[256,128]{1,0:T(8,128)S(1)} %get-tuple-element.28), channel_id=1, source_target_pairs={{0,6},{1,7},{2,0},{3,1},{4,2},{5,3},{6,4},{7,5},{8,14},{9,15},{10,... | collective-permute-start | bytes 393224 | tf_op jit(solution)/shard_map/ppermute | solution.py:348
  104.6 10.8 %collective-permute-start.13 = (f32[512,128]{1,0:T(8,128)S(1)}, f32[512,128]{1,0:T(8,128)S(1)}, u32[]{:S(2)}, u32[]{:S(2)}) collective-permute-start(f32[512,128]{1,0:T(8,128)S(1)} %shard_map.52.after_ref), channel_id=1, source_target_pairs={{0,2},{1,3},{2,4},{3,5},{4,6},{5,7},{6,0},{7,1},{8,10},{9,11},{10,... | collective-permute-start | bytes 786440 | tf_op jit(solution)/shard_map/ppermute | solution.py:348
  113.4 17.8 %collective-permute-start.15 = (f32[512,128]{1,0:T(8,128)S(1)}, f32[512,128]{1,0:T(8,128)S(1)}, u32[]{:S(2)}, u32[]{:S(2)}) collective-permute-start(f32[512,128]{1,0:T(8,128)S(1)} %shard_map.54), channel_id=1, source_target_pairs={{0,6},{1,7},{2,0},{3,1},{4,2},{5,3},{6,4},{7,5},{8,14},{9,15},{10,... | collective-permute-start | bytes 786440 | tf_op jit(solution)/shard_map/ppermute | solution.py:348

commit v5 on v4

--- a/solution.py
+++ b/solution.py
@@ -365,9 +365,10 @@
     r3 = swap_z(r2, 1)
     s1, s2 = swap_core(r1), swap_core(r2)
     ls = split_others(where, ls, xs)
-    r3, ls = lax.optimization_barrier((r3, ls))
+    s3 = swap_core(r3)
+    s2, ls = lax.optimization_barrier((s2, ls))
     rs = first_right(where, r, sibling, r1, r2, s1, s2)
-    rs = last_right(where, rs, r3, swap_core(r3))
+    rs = last_right(where, rs, r3, s3)
     p3 = shares(where, tab, ls, rs, (3, 1), where)
     m3 = shares(where, tab, ls, rs, (-3, -1), p3)
     f0, f1 = far(where, tab, ls, rs, m3)

time: 133 us -> 132 us (level)
  the two profiles are of different devices: /device:TPU:209 before, /device:TPU:1 now
where the time goes in v5:
time: 132 us; the launch traced here: 130 us
  starting transfers between devices  83.8 us (63%)
  Pallas kernels  22.5 us (17%)
  waiting for transfers between devices  20.1 us (15%)
  local copies, waits for them, and re-layouts  3.38 us (3%)
    ppermute x6, starting transfers between devices, along_depth(): lax.ppermute(x, 'depth', [(i, (i + k) % LAYERS) for i in range(LAYERS)])  21.9 us
    ppermute x3, starting transfers between devices, swap_z(): return lax.ppermute(x, 'row', [(i, i ^ 2 * k) for i in range(8)])  20.1 us
    ppermute x6, waiting for transfers between devices, along_depth(): lax.ppermute(x, 'depth', [(i, (i + k) % LAYERS) for i in range(LAYERS)])  19.2 us
    all_to_all x2, starting transfers between devices, to_group(): return lax.all_to_all(x, axis, 0, 0, axis_index_groups=groups)  18.9 us
    ppermute x4, starting transfers between devices, swap_core(): return lax.ppermute(x, 'row', [(i, i ^ 1) for i in range(8)])  12.3 us
    ppermute x3, starting transfers between devices, along_x(): lax.ppermute(x, 'col', [(z * 4 + c, z * 4 + (c + k) % 4) for z in range(3...  10.5 us
    pallas_call x1, Pallas kernels, table(): pl.pallas_call(table_kernel, out_shape=jax.ShapeDtypeStruct((136,), jnp.i...  4.94 us
    pallas_call x3, Pallas kernels, shares(): pl.pallas_call(kernel, out_shape=jax.ShapeDtypeStruct((512 * len(offsets)...  4.25 us
  transfers between devices with their start and end apart: 18, of which 5 were waited for; matrix products, arithmetic and copies ran while one was open for 0% of the time, Pallas kernels for 13%

profile of v5, /device:TPU:1, one launch (start us, length us, event | category | flops | bytes accessed | tf_op | source)
XLA Modules:
  0.0 130.2 jit_solution(13399600868835384580)
XLA Ops:
  0.0 1.0 copy-done.2
  1.0 1.1 shard_map.37
  2.2 14.5 %all-to-all-start = ((f32[3,256,256]{2,1,0:T(8,128)}), f32[3,256,256]{2,1,0:T(8,128)}, u32[]{:S(2)}, u32[]{:S(2)}) async-start(f32[3,256,256]{2,1,0:T(8,128)} %get-tuple-element.17), calls=%async_computation | async-start | bytes 1572864 | tf_op jit(solution)/shard_map/all_to_all | solution.py:328
  16.6 3.1 %collective-permute-start.2 = (f32[256,256]{1,0:T(8,128)}, f32[256,256]{1,0:T(8,128)}, u32[]{:S(2)}, u32[]{:S(2)}) collective-permute-start(f32[256,256]{1,0:T(8,128)} %get-tuple-element.18.part), channel_id=1, source_target_pairs={{0,8},{8,16},{16,24},{24,0},{32,40},{40,48},{48,56},{56,32},{64,72... | collective-permute-start | bytes 786440 | tf_op jit(solution)/shard_map/ppermute | solution.py:336
  19.7 4.4 %collective-permute-start.1 = (f32[256,256]{1,0:T(8,128)}, f32[256,256]{1,0:T(8,128)}, u32[]{:S(2)}, u32[]{:S(2)}) collective-permute-start(f32[256,256]{1,0:T(8,128)} %get-tuple-element.18.part), channel_id=1, source_target_pairs={{0,16},{8,24},{16,0},{24,8},{32,48},{40,56},{48,32},{56,40},{64,80... | collective-permute-start | bytes 786440 | tf_op jit(solution)/shard_map/ppermute | solution.py:336
  24.1 3.1 %collective-permute-start = (f32[256,256]{1,0:T(8,128)}, f32[256,256]{1,0:T(8,128)}, u32[]{:S(2)}, u32[]{:S(2)}) collective-permute-start(f32[256,256]{1,0:T(8,128)} %get-tuple-element.18.part), channel_id=1, source_target_pairs={{0,24},{8,0},{16,8},{24,16},{32,56},{40,32},{48,40},{56,48},{64,88... | collective-permute-start | bytes 786440 | tf_op jit(solution)/shard_map/ppermute | solution.py:336
  27.2 0.0 copy-start.1
  27.2 1.0 copy-done.1
  28.2 0.1 shard_map.42.r
  28.4 3.7 %collective-permute-start.3 = (f32[256,256]{1,0:T(8,128)S(1)}, f32[256,256]{1,0:T(8,128)}, u32[]{:S(2)}, u32[]{:S(2)}) collective-permute-start(f32[256,256]{1,0:T(8,128)S(1)} %shard_map.42.r), channel_id=1, source_target_pairs={{0,96},{96,0},{192,288},{288,192},{384,480},{480,384},{576,672},{6... | collective-permute-start | bytes 786440 | tf_op jit(solution)/shard_map/ppermute | solution.py:344
  32.1 0.1 pad_add_fusion.where.after_ref
  32.2 1.0 shard_map.38.rest_0_
  33.2 4.9 %shard_map.43.tab = s32[136]{0:T(256)S(1)} custom-call(s32[3,512]{1,0:T(4,128)S(1)} %copy-done.3), custom_call_target="tpu_custom_call" | custom-call | bytes 8388608 | tf_op jit(solution)/shard_map/pallas_call | solution.py:86
  38.1 1.0 shard_map.39.rest_0_
  39.1 0.0 collective-permute-done.1.part
  39.1 1.0 shard_map.40.rest_0_
  40.1 0.0 collective-permute-done.part
  40.1 1.0 shard_map.41.ls_in
  41.2 1.3 shard_map.44
  42.5 1.3 copy-done
  43.8 4.5 %all-to-all-start.1 = ((f32[4,512,256]{2,1,0:T(8,128)}), f32[4,512,256]{2,1,0:T(8,128)}, u32[]{:S(2)}, u32[]{:S(2)}) async-start(f32[4,512,256]{2,1,0:T(8,128)} %copy-done), calls=%async_computation.1 | async-start | bytes 4194304 | tf_op jit(solution)/shard_map/all_to_all | solution.py:328
  48.2 5.4 %collective-permute-start.4 = (f32[256,256]{1,0:T(8,128)S(1)}, f32[256,256]{1,0:T(8,128)}, u32[]{:S(2)}, u32[]{:S(2)}) collective-permute-start(f32[256,256]{1,0:T(8,128)S(1)} %shard_map.42.r), channel_id=1, source_target_pairs={{0,384},{96,480},{192,576},{288,672},{384,0},{480,96},{576,192},{6... | collective-permute-start | bytes 786440 | tf_op jit(solution)/shard_map/ppermute | solution.py:340
  53.6 6.5 %collective-permute-start.6 = (f32[256,256]{1,0:T(8,128)S(1)}, f32[256,256]{1,0:T(8,128)}, u32[]{:S(2)}, u32[]{:S(2)}) collective-permute-start(f32[256,256]{1,0:T(8,128)S(1)} %shard_map.42.r), channel_id=1, source_target_pairs={{0,192},{96,288},{192,0},{288,96},{384,576},{480,672},{576,384},{6... | collective-permute-start | bytes 786440 | tf_op jit(solution)/shard_map/ppermute | solution.py:340
  60.1 8.3 %collective-permute-start.8 = (f32[256,256]{1,0:T(8,128)}, f32[256,256]{1,0:T(8,128)}, u32[]{:S(2)}, u32[]{:S(2)}) collective-permute-start(f32[256,256]{1,0:T(8,128)} %collective-permute-done.4.r2), channel_id=1, source_target_pairs={{0,192},{96,288},{192,0},{288,96},{384,576},{480,672},{576,384},{6... | collective-permute-start | bytes 786440 | tf_op jit(solution)/shard_map/ppermute | solution.py:340
  68.4 2.7 %collective-permute-start.5 = (f32[256,256]{1,0:T(8,128)}, f32[256,256]{1,0:T(8,128)}, u32[]{:S(2)}, u32[]{:S(2)}) collective-permute-start(f32[256,256]{1,0:T(8,128)} %collective-permute-done.4.r2), channel_id=1, source_target_pairs={{0,96},{96,0},{192,288},{288,192},{384,480},{480,384},{576,672},{6... | collective-permute-start | bytes 786440 | tf_op jit(solution)/shard_map/ppermute | solution.py:344
  71.1 1.9 %collective-permute-start.7 = (f32[256,256]{1,0:T(8,128)}, f32[256,256]{1,0:T(8,128)}, u32[]{:S(2)}, u32[]{:S(2)}) collective-permute-start(f32[256,256]{1,0:T(8,128)} %collective-permute-done.6.r1), channel_id=1, source_target_pairs={{0,96},{96,0},{192,288},{288,192},{384,480},{480,384},{576,672},{6... | collective-permute-start | bytes 786440 | tf_op jit(solution)/shard_map/ppermute | solution.py:344
  73.0 0.9 collective-permute-done.8.r3
  73.9 4.0 %collective-permute-start.9 = (f32[256,256]{1,0:T(8,128)}, f32[256,256]{1,0:T(8,128)}, u32[]{:S(2)}, u32[]{:S(2)}) collective-permute-start(f32[256,256]{1,0:T(8,128)} %collective-permute-done.8.r3), channel_id=1, source_target_pairs={{0,96},{96,0},{192,288},{288,192},{384,480},{480,384},{576,672},{6... | collective-permute-start | bytes 786440 | tf_op jit(solution)/shard_map/ppermute | solution.py:344
  77.9 1.8 %shard_map.45.ls = bf16[48,128,256]{2,1,0:T(8,128)(2,1)S(1)} custom-call(s32[3]{0:T(128)S(1)} %pad_add_fusion.where.after_ref, bf16[48,128,256]{2,1,0:T(8,128)(2,1)S(1)} %shard_map.41.ls_in, f32[4,512,256]{2,1,0:T(8,128)} %all-to-all-done.1.xs), custom_call_target="tpu_custom_call", output_to_operand_aliasing={{}: (1, {})} | custom-call | bytes 4194304 | tf_op jit(solution)/shard_map/pallas_call | solution.py:186
  79.7 1.7 %shard_map.46.rs_in = bf16[32,256,128]{2,1,0:T(8,128)(2,1)S(1)} custom-call(s32[3]{0:T(128)S(1)} %pad_add_fusion.where.after_ref, f32[256,256]{1,0:T(8,128)S(1)} %shard_map.42.r, f32[256,256]{1,0:T(8,128)} %collective-permute-done.3.sibling, f32[256,256]{1,0:T(8,128)} %collective-permute-done.6.r1, f32[256,256]{1,0:T(8,128)} %collective-permute-done.4.r2, ...), custom_call_target="tpu_custom_call" | custom-call | bytes 4194304 | tf_op jit(solution)/shard_map/pallas_call | solution.py:208
  81.4 1.2 shard_map.47.rs
  82.6 1.3 %shard_map.48.after_ref = f32[1024,128]{1,0:T(8,128)S(1)} custom-call(s32[3]{0:T(128)S(1)} %pad_add_fusion.where.after_ref, s32[136]{0:T(256)S(1)} %shard_map.43.tab, bf16[48,128,256]{2,1,0:T(8,128)(2,1)S(1)} %shard_map.45.ls, bf16[32,256,128]{2,1,0:T(8,128)(2,1)S(1)} %shard_map.47.rs, s32[3]{0:T(128)S(1)} %pad_add_fusion.where.after_ref), custom_call_target="tpu_custom_call" | custom-call | flops 268435456 | bytes 2097152 | tf_op jit(solution)/shard_map/pallas_call | solution.py:245
  83.9 3.2 %collective-permute-start.10 = (f32[1024,128]{1,0:T(8,128)S(1)}, f32[1024,128]{1,0:T(8,128)S(1)}, u32[]{:S(2)}, u32[]{:S(2)}) collective-permute-start(f32[1024,128]{1,0:T(8,128)S(1)} %shard_map.48.after_ref), channel_id=1, source_target_pairs={{0,1},{1,2},{2,3},{3,4},{4,5},{5,6},{6,7},{7,0},{8,9},{9,10},{10,1... | collective-permute-start | bytes 1572872 | tf_op jit(solution)/shard_map/ppermute | solution.py:348
  87.1 1.3 %shard_map.49.after_ref = f32[1024,128]{1,0:T(8,128)S(1)} custom-call(s32[3]{0:T(128)S(1)} %pad_add_fusion.where.after_ref, s32[136]{0:T(256)S(1)} %shard_map.43.tab, bf16[48,128,256]{2,1,0:T(8,128)(2,1)S(1)} %shard_map.45.ls, bf16[32,256,128]{2,1,0:T(8,128)(2,1)S(1)} %shard_map.47.rs, f32[1024,128]{1,0:T(8,128)S(1)} %shard_map.48.after_ref), custom_call_target="tpu_custom_call" | custom-call | flops 268435456 | bytes 2097152 | tf_op jit(solution)/shard_map/pallas_call | solution.py:245
  88.5 3.8 %collective-permute-start.11 = (f32[1024,128]{1,0:T(8,128)S(1)}, f32[1024,128]{1,0:T(8,128)S(1)}, u32[]{:S(2)}, u32[]{:S(2)}) collective-permute-start(f32[1024,128]{1,0:T(8,128)S(1)} %shard_map.49.after_ref), channel_id=1, source_target_pairs={{0,7},{1,0},{2,1},{3,2},{4,3},{5,4},{6,5},{7,6},{8,15},{9,8},{10,9... | collective-permute-start | bytes 1572872 | tf_op jit(solution)/shard_map/ppermute | solution.py:348
  92.3 1.1 shard_map.50
  93.3 2.5 %collective-permute-start.12 = (f32[256,128]{1,0:T(8,128)S(1)}, f32[256,128]{1,0:T(8,128)S(1)}, u32[]{:S(2)}, u32[]{:S(2)}) collective-permute-start(f32[256,128]{1,0:T(8,128)S(1)} %get-tuple-element.27.after_ref), channel_id=1, source_target_pairs={{0,2},{1,3},{2,4},{3,5},{4,6},{5,7},{6,0},{7,1},{8,10},{9,11},{10,... | collective-permute-start | bytes 393224 | tf_op jit(solution)/shard_map/ppermute | solution.py:348
  95.8 4.9 %collective-permute-start.14 = (f32[256,128]{1,0:T(8,128)S(1)}, f32[256,128]{1,0:T(8,128)S(1)}, u32[]{:S(2)}, u32[]{:S(2)}) collective-permute-start(f32[256,128]{1,0:T(8,128)S(1)} %get-tuple-element.28), channel_id=1, source_target_pairs={{0,6},{1,7},{2,0},{3,1},{4,2},{5,3},{6,4},{7,5},{8,14},{9,15},{10,... | collective-permute-start | bytes 393224 | tf_op jit(solution)/shard_map/ppermute | solution.py:348
  100.7 1.6 %shard_map.51.near = f32[1536,128]{1,0:T(8,128)S(1)} custom-call(s32[3]{0:T(128)S(1)} %pad_add_fusion.where.after_ref, s32[136]{0:T(256)S(1)} %shard_map.43.tab, bf16[48,128,256]{2,1,0:T(8,128)(2,1)S(1)} %shard_map.45.ls, bf16[32,256,128]{2,1,0:T(8,128)(2,1)S(1)} %shard_map.47.rs, f32[256,128]{1,0:T(8,128)S(1)} %get-tuple-element.27.after_ref), custom_call_target="tpu_custom_call" | custom-call | flops 402653184 | bytes 3145728 | tf_op jit(solution)/shard_map/pallas_call | solution.py:245
  102.3 3.6 %collective-permute-done.12.half = f32[256,128]{1,0:T(8,128)S(1)} collective-permute-done((f32[256,128]{1,0:T(8,128)S(1)}, f32[256,128]{1,0:T(8,128)S(1)}, u32[]{:S(2)}, u32[]{:S(2)}) %collective-permute-start.12) | collective-permute-done | bytes 131104 | tf_op jit(solution)/shard_map/ppermute | solution.py:348
  106.0 2.0 %collective-permute-start.13 = (f32[512,128]{1,0:T(8,128)S(1)}, f32[512,128]{1,0:T(8,128)S(1)}, u32[]{:S(2)}, u32[]{:S(2)}) collective-permute-start(f32[512,128]{1,0:T(8,128)S(1)} %shard_map.52.after_ref), channel_id=1, source_target_pairs={{0,2},{1,3},{2,4},{3,5},{4,6},{5,7},{6,0},{7,1},{8,10},{9,11},{10,... | collective-permute-start | bytes 786440 | tf_op jit(solution)/shard_map/ppermute | solution.py:348
  108.0 1.9 %collective-permute-done.14.half = f32[256,128]{1,0:T(8,128)S(1)} collective-permute-done((f32[256,128]{1,0:T(8,128)S(1)}, f32[256,128]{1,0:T(8,128)S(1)}, u32[]{:S(2)}, u32[]{:S(2)}) %collective-permute-start.14) | collective-permute-done | bytes 131104 | tf_op jit(solution)/shard_map/ppermute | solution.py:348
  109.9 0.1 shard_map.54
  109.9 5.6 %collective-permute-start.15 = (f32[512,128]{1,0:T(8,128)S(1)}, f32[512,128]{1,0:T(8,128)S(1)}, u32[]{:S(2)}, u32[]{:S(2)}) collective-permute-start(f32[512,128]{1,0:T(8,128)S(1)} %shard_map.54), channel_id=1, source_target_pairs={{0,6},{1,7},{2,0},{3,1},{4,2},{5,3},{6,4},{7,5},{8,14},{9,15},{10,... | collective-permute-start | bytes 786440 | tf_op jit(solution)/shard_map/ppermute | solution.py:348
  115.5 1.6 %collective-permute-done.13.u = f32[512,128]{1,0:T(8,128)S(1)} collective-permute-done((f32[512,128]{1,0:T(8,128)S(1)}, f32[512,128]{1,0:T(8,128)S(1)}, u32[]{:S(2)}, u32[]{:S(2)}) %collective-permute-start.13) | collective-permute-done | bytes 262176 | tf_op jit(solution)/shard_map/ppermute | solution.py:348
  117.1 0.1 shard_map.53.part
  117.2 12.0 %collective-permute-done.15.d = f32[512,128]{1,0:T(8,128)S(1)} collective-permute-done((f32[512,128]{1,0:T(8,128)S(1)}, f32[512,128]{1,0:T(8,128)S(1)}, u32[]{:S(2)}, u32[]{:S(2)}) %collective-permute-start.15) | collective-permute-done | bytes 262176 | tf_op jit(solution)/shard_map/ppermute | solution.py:348
  129.2 0.9 shard_map.55
  (16 shorter events, 0.1 us)
Async XLA Ops:
  0.0 1.0 copy-start.2
  1.0 32.1 %copy-start.3 = (s32[3,512]{1,0:T(4,128)S(1)}, s32[3,512]{1,0:T(4,128)}, u32[]{:S(2)}) copy-start(s32[3,512]{1,0:T(4,128)} %t_ref.1) | copy-start | bytes 18436
  2.2 39.0 %all-to-all-start = ((f32[3,256,256]{2,1,0:T(8,128)}), f32[3,256,256]{2,1,0:T(8,128)}, u32[]{:S(2)}, u32[]{:S(2)}) async-start(f32[3,256,256]{2,1,0:T(8,128)} %get-tuple-element.17), calls=%async_computation | async-start | bytes 1572864 | tf_op jit(solution)/shard_map/all_to_all | solution.py:328
  16.6 21.5 %collective-permute-start.2 = (f32[256,256]{1,0:T(8,128)}, f32[256,256]{1,0:T(8,128)}, u32[]{:S(2)}, u32[]{:S(2)}) collective-permute-start(f32[256,256]{1,0:T(8,128)} %get-tuple-element.18.part), channel_id=1, source_target_pairs={{0,8},{8,16},{16,24},{24,0},{32,40},{40,48},{48,56},{56,32},{64,72... | collective-permute-start | bytes 786440 | tf_op jit(solution)/shard_map/ppermute | solution.py:336
  19.7 19.4 %collective-permute-start.1 = (f32[256,256]{1,0:T(8,128)}, f32[256,256]{1,0:T(8,128)}, u32[]{:S(2)}, u32[]{:S(2)}) collective-permute-start(f32[256,256]{1,0:T(8,128)} %get-tuple-element.18.part), channel_id=1, source_target_pairs={{0,16},{8,24},{16,0},{24,8},{32,48},{40,56},{48,32},{56,40},{64,80... | collective-permute-start | bytes 786440 | tf_op jit(solution)/shard_map/ppermute | solution.py:336
  24.1 16.0 %collective-permute-start = (f32[256,256]{1,0:T(8,128)}, f32[256,256]{1,0:T(8,128)}, u32[]{:S(2)}, u32[]{:S(2)}) collective-permute-start(f32[256,256]{1,0:T(8,128)} %get-tuple-element.18.part), channel_id=1, source_target_pairs={{0,24},{8,0},{16,8},{24,16},{32,56},{40,32},{48,40},{56,48},{64,88... | collective-permute-start | bytes 786440 | tf_op jit(solution)/shard_map/ppermute | solution.py:336
  27.2 1.0 copy-start.1
  28.4 12.8 %collective-permute-start.3 = (f32[256,256]{1,0:T(8,128)S(1)}, f32[256,256]{1,0:T(8,128)}, u32[]{:S(2)}, u32[]{:S(2)}) collective-permute-start(f32[256,256]{1,0:T(8,128)S(1)} %shard_map.42.r), channel_id=1, source_target_pairs={{0,96},{96,0},{192,288},{288,192},{384,480},{480,384},{576,672},{6... | collective-permute-start | bytes 786440 | tf_op jit(solution)/shard_map/ppermute | solution.py:344
  42.5 1.3 %copy-start = (f32[4,512,256]{2,1,0:T(8,128)}, f32[4,512,256]{2,1,0:T(8,128)S(1)}, u32[]{:S(2)}) copy-start(f32[4,512,256]{2,1,0:T(8,128)S(1)} %shard_map.44) | copy-start | bytes 6291460
  43.8 34.1 %all-to-all-start.1 = ((f32[4,512,256]{2,1,0:T(8,128)}), f32[4,512,256]{2,1,0:T(8,128)}, u32[]{:S(2)}, u32[]{:S(2)}) async-start(f32[4,512,256]{2,1,0:T(8,128)} %copy-done), calls=%async_computation.1 | async-start | bytes 4194304 | tf_op jit(solution)/shard_map/all_to_all | solution.py:328
  48.2 11.8 %collective-permute-start.4 = (f32[256,256]{1,0:T(8,128)S(1)}, f32[256,256]{1,0:T(8,128)}, u32[]{:S(2)}, u32[]{:S(2)}) collective-permute-start(f32[256,256]{1,0:T(8,128)S(1)} %shard_map.42.r), channel_id=1, source_target_pairs={{0,384},{96,480},{192,576},{288,672},{384,0},{480,96},{576,192},{6... | collective-permute-start | bytes 786440 | tf_op jit(solution)/shard_map/ppermute | solution.py:340
  53.6 17.5 %collective-permute-start.6 = (f32[256,256]{1,0:T(8,128)S(1)}, f32[256,256]{1,0:T(8,128)}, u32[]{:S(2)}, u32[]{:S(2)}) collective-permute-start(f32[256,256]{1,0:T(8,128)S(1)} %shard_map.42.r), channel_id=1, source_target_pairs={{0,192},{96,288},{192,0},{288,96},{384,576},{480,672},{576,384},{6... | collective-permute-start | bytes 786440 | tf_op jit(solution)/shard_map/ppermute | solution.py:340
  60.1 13.8 %collective-permute-start.8 = (f32[256,256]{1,0:T(8,128)}, f32[256,256]{1,0:T(8,128)}, u32[]{:S(2)}, u32[]{:S(2)}) collective-permute-start(f32[256,256]{1,0:T(8,128)} %collective-permute-done.4.r2), channel_id=1, source_target_pairs={{0,192},{96,288},{192,0},{288,96},{384,576},{480,672},{576,384},{6... | collective-permute-start | bytes 786440 | tf_op jit(solution)/shard_map/ppermute | solution.py:340
  68.4 11.3 %collective-permute-start.5 = (f32[256,256]{1,0:T(8,128)}, f32[256,256]{1,0:T(8,128)}, u32[]{:S(2)}, u32[]{:S(2)}) collective-permute-start(f32[256,256]{1,0:T(8,128)} %collective-permute-done.4.r2), channel_id=1, source_target_pairs={{0,96},{96,0},{192,288},{288,192},{384,480},{480,384},{576,672},{6... | collective-permute-start | bytes 786440 | tf_op jit(solution)/shard_map/ppermute | solution.py:344
  71.1 8.6 %collective-permute-start.7 = (f32[256,256]{1,0:T(8,128)}, f32[256,256]{1,0:T(8,128)}, u32[]{:S(2)}, u32[]{:S(2)}) collective-permute-start(f32[256,256]{1,0:T(8,128)} %collective-permute-done.6.r1), channel_id=1, source_target_pairs={{0,96},{96,0},{192,288},{288,192},{384,480},{480,384},{576,672},{6... | collective-permute-start | bytes 786440 | tf_op jit(solution)/shard_map/ppermute | solution.py:344
  73.9 7.5 %collective-permute-start.9 = (f32[256,256]{1,0:T(8,128)}, f32[256,256]{1,0:T(8,128)}, u32[]{:S(2)}, u32[]{:S(2)}) collective-permute-start(f32[256,256]{1,0:T(8,128)} %collective-permute-done.8.r3), channel_id=1, source_target_pairs={{0,96},{96,0},{192,288},{288,192},{384,480},{480,384},{576,672},{6... | collective-permute-start | bytes 786440 | tf_op jit(solution)/shard_map/ppermute | solution.py:344
  83.9 22.0 %collective-permute-start.10 = (f32[1024,128]{1,0:T(8,128)S(1)}, f32[1024,128]{1,0:T(8,128)S(1)}, u32[]{:S(2)}, u32[]{:S(2)}) collective-permute-start(f32[1024,128]{1,0:T(8,128)S(1)} %shard_map.48.after_ref), channel_id=1, source_target_pairs={{0,1},{1,2},{2,3},{3,4},{4,5},{5,6},{6,7},{7,0},{8,9},{9,10},{10,1... | collective-permute-start | bytes 1572872 | tf_op jit(solution)/shard_map/ppermute | solution.py:348
  88.5 21.4 %collective-permute-start.11 = (f32[1024,128]{1,0:T(8,128)S(1)}, f32[1024,128]{1,0:T(8,128)S(1)}, u32[]{:S(2)}, u32[]{:S(2)}) collective-permute-start(f32[1024,128]{1,0:T(8,128)S(1)} %shard_map.49.after_ref), channel_id=1, source_target_pairs={{0,7},{1,0},{2,1},{3,2},{4,3},{5,4},{6,5},{7,6},{8,15},{9,8},{10,9... | collective-permute-start | bytes 1572872 | tf_op jit(solution)/shard_map/ppermute | solution.py:348
  93.3 12.6 %collective-permute-start.12 = (f32[256,128]{1,0:T(8,128)S(1)}, f32[256,128]{1,0:T(8,128)S(1)}, u32[]{:S(2)}, u32[]{:S(2)}) collective-permute-start(f32[256,128]{1,0:T(8,128)S(1)} %get-tuple-element.27.after_ref), channel_id=1, source_target_pairs={{0,2},{1,3},{2,4},{3,5},{4,6},{5,7},{6,0},{7,1},{8,10},{9,11},{10,... | collective-permute-start | bytes 393224 | tf_op jit(solution)/shard_map/ppermute | solution.py:348
  95.8 14.0 %collective-permute-start.14 = (f32[256,128]{1,0:T(8,128)S(1)}, f32[256,128]{1,0:T(8,128)S(1)}, u32[]{:S(2)}, u32[]{:S(2)}) collective-permute-start(f32[256,128]{1,0:T(8,128)S(1)} %get-tuple-element.28), channel_id=1, source_target_pairs={{0,6},{1,7},{2,0},{3,1},{4,2},{5,3},{6,4},{7,5},{8,14},{9,15},{10,... | collective-permute-start | bytes 393224 | tf_op jit(solution)/shard_map/ppermute | solution.py:348
  106.0 11.1 %collective-permute-start.13 = (f32[512,128]{1,0:T(8,128)S(1)}, f32[512,128]{1,0:T(8,128)S(1)}, u32[]{:S(2)}, u32[]{:S(2)}) collective-permute-start(f32[512,128]{1,0:T(8,128)S(1)} %shard_map.52.after_ref), channel_id=1, source_target_pairs={{0,2},{1,3},{2,4},{3,5},{4,6},{5,7},{6,0},{7,1},{8,10},{9,11},{10,... | collective-permute-start | bytes 786440 | tf_op jit(solution)/shard_map/ppermute | solution.py:348
  109.9 19.3 %collective-permute-start.15 = (f32[512,128]{1,0:T(8,128)S(1)}, f32[512,128]{1,0:T(8,128)S(1)}, u32[]{:S(2)}, u32[]{:S(2)}) collective-permute-start(f32[512,128]{1,0:T(8,128)S(1)} %shard_map.54), channel_id=1, source_target_pairs={{0,6},{1,7},{2,0},{3,1},{4,2},{5,3},{6,4},{7,5},{8,14},{9,15},{10,... | collective-permute-start | bytes 786440 | tf_op jit(solution)/shard_map/ppermute | solution.py:348
